TPU v7x, 32 devices: a whole 2x2x4 slice. The times are simulated.
32 devices in a mesh: dp: 4 (over x, core), seq: 8 (over z, y).
Axes of the slice: x: 2, y: 2, z: 4, core: 2. Of those that a mesh axis runs over, the one named last changes fastest.
Arguments:
- tokens: bfloat16 [4, 4096, 1280], P('dp', 'seq'), may hold values from -6 to 6
- bounds: int32 [2, 4, 4096], P(None, 'dp', 'seq'), may hold values from 0 to 4095, as said below
- w_in: bfloat16 [2, 1280, 640], replicated, may hold values from -0.15625 to 0.15625
- w_mid: bfloat16 [2, 5, 640, 640], replicated, may hold values from -0.109375 to 0.109375
- w_out: bfloat16 [2, 640, 1280], replicated, may hold values from -0.25 to 0.25
- gain_wide: float32 [2, 1280], replicated, may hold values from 0.25 to 1.75
- shift_wide: float32 [2, 1280], replicated, may hold values from -1.5 to 1.5
- gain_narrow: float32 [2, 2, 640], replicated, may hold values from 0.25 to 1.75
- shift_narrow: float32 [2, 2, 640], replicated, may hold values from -1.5 to 1.5
- bias_narrow: float32 [2, 2, 640], replicated, may hold values from -1.5 to 1.5
- bias_wide: float32 [2, 1280], replicated, may hold values from -1.5 to 1.5
- cotangent: bfloat16 [4, 4096, 1280], P('dp', 'seq'), may hold values from -6 to 6
Outputs:
- out: float32 [4, 4096, 1280], P('dp', 'seq')
- grad_tokens: float32 [4, 4096, 1280], P('dp', 'seq')
- grad_w_in: float32 [2, 1280, 640], P(None, 'seq')
- grad_w_mid: float32 [2, 5, 640, 640], P(None, None, None, 'seq')
- grad_w_out: float32 [2, 640, 1280], P(None, None, 'seq')
- grad_gain_wide: float32 [2, 1280], replicated
- grad_shift_wide: float32 [2, 1280], replicated
- grad_gain_narrow: float32 [2, 2, 640], replicated
- grad_shift_narrow: float32 [2, 2, 640], replicated
- grad_bias_narrow: float32 [2, 2, 640], replicated
- grad_bias_wide: float32 [2, 1280], replicated
Inputs may be any that keep to these rules, and one draw needn't show every extreme that they name: bounds[0] and bounds[1] give, for each token, the first position and one past the last position of its protein in its row. Proteins are contiguous and follow one another from position 0; each run of 512 positions starting at a multiple of 512 holds exactly one protein end, at least 128 and less than 384 into the run; after the last protein end the row is padding, where both entries equal the token's own position (an empty protein).
All inputs are finite; a program needn't handle non-finite values.
Results may differ from a plain program's by a relative error of at most 0.015.
Values may be sent and summed in bfloat16 or wider, within the bound.
No kernel may reach another device: no remote copies, remote signals or barrier semaphores. Data moves between devices by JAX's collectives and lax.ppermute only.
A program may use at most 256 MiB of HBM per device.

v0:
```python
import jax
import jax.numpy as jnp
from jax import lax
from jax.sharding import PartitionSpec as P

DILATION_CLOSE = 4
DILATION_BROAD = 128
BLOCKS = 2


def padded_2(x, sides, width):
    for axis, dim in sides:
        count, length = (lax.axis_size(axis), x.shape[dim])
        up = [(i, (i + 1) % count) for i in range(count - 1)]
        down = [(j, i) for i, j in up]
        last = lax.slice_in_dim(x, length - width, length, axis=dim)
        first = lax.slice_in_dim(x, 0, width, axis=dim)
        before = lax.ppermute(last, axis, up)
        after = lax.ppermute(first, axis, down)
        x = jnp.concatenate([before, x, after], axis=dim)
    return x


def from_behind(x, axis, by):
    count = lax.axis_size(axis)
    pairs = [(i, i + by) for i in range(count) if 0 <= i + by < count]
    return lax.ppermute(x, axis, pairs)


def norm_act(values, gain_row, shift_row):
    average = jnp.mean(values, axis=-1, keepdims=True)
    centred = values - average
    inverse = lax.rsqrt(jnp.mean(centred * centred, axis=-1, keepdims=True) + 1e-05)
    return jax.nn.gelu(centred * inverse * gain_row + shift_row, approximate=False)


def make_masks(starts, end_points, position, dilation_step, tap_count):
    offsets = (jnp.arange(tap_count, dtype=jnp.int32) - tap_count // 2) * dilation_step
    target = position[None, :] + offsets[:, None]
    inside = (starts[None, :] <= target) & (target < end_points[None, :])
    return inside.astype(jnp.float32)


def along_rows(left, right):
    return lax.dot_general(
        left, right, (((1,), (1,)), ((), ())), preferred_element_type=jnp.float32
    )


def over_tokens(left, right):
    return lax.dot_general(
        left, right, (((0,), (0,)), ((), ())), preferred_element_type=jnp.float32
    )


def body(
    tokens,
    bounds,
    w_in,
    w_mid,
    w_out,
    gain_wide,
    shift_wide,
    gain_narrow,
    shift_narrow,
    bias_narrow,
    bias_wide,
    cotangent,
):
    tok_rows = tokens.shape[1]
    tap_count = w_mid.shape[1]
    position = lax.axis_index("seq") * tok_rows + jnp.arange(tok_rows, dtype=jnp.int32)
    starts = bounds[0, 0]
    end_points = bounds[1, 0]
    current = tokens[0].astype(jnp.float32)
    saved_state = []
    for index_of_block in range(BLOCKS):
        dilation_step = DILATION_CLOSE if index_of_block == 0 else DILATION_BROAD
        rim_width = 2 * dilation_step
        tap_masks = make_masks(starts, end_points, position, dilation_step, tap_count)
        act_one, back_one = jax.vjp(
            norm_act, current, gain_wide[index_of_block], shift_wide[index_of_block]
        )
        act_one = act_one.astype(jnp.bfloat16)
        inner_one = (
            jnp.dot(act_one, w_in[index_of_block], preferred_element_type=jnp.float32)
            + bias_narrow[index_of_block, 0]
        )
        second_activation, back_two = jax.vjp(
            norm_act, inner_one, gain_narrow[index_of_block, 0], shift_narrow[index_of_block, 0]
        )
        second_activation = second_activation.astype(jnp.bfloat16)
        if index_of_block == 0:
            padded = padded_2(second_activation, (("seq", 0),), rim_width)
        else:
            padded = padded_2(second_activation, (("seq", 0),), rim_width)
        mixed = bias_narrow[index_of_block, 1]
        for tap_index in range(tap_count):
            window = padded[tap_index * dilation_step : tap_index * dilation_step + tok_rows]
            mixed = mixed + tap_masks[tap_index][:, None] * jnp.dot(
                window, w_mid[index_of_block, tap_index], preferred_element_type=jnp.float32
            )
        third_activation, third_backward = jax.vjp(
            norm_act, mixed, gain_narrow[index_of_block, 1], shift_narrow[index_of_block, 1]
        )
        third_activation = third_activation.astype(jnp.bfloat16)
        current = (
            current
            + jnp.dot(third_activation, w_out[index_of_block], preferred_element_type=jnp.float32)
            + bias_wide[index_of_block]
        )
        saved_state.append(
            (tap_masks, act_one, padded, third_activation, back_one, back_two, third_backward)
        )
    grad_flow = cotangent[0].astype(jnp.float32)
    weight_sums = [None] * BLOCKS
    vector_sums = [None] * BLOCKS
    for index_of_block in reversed(range(BLOCKS)):
        tap_masks, act_one, padded, third_activation, back_one, back_two, third_backward = (
            saved_state[index_of_block]
        )
        dilation_step = DILATION_CLOSE if index_of_block == 0 else DILATION_BROAD
        rim_width = 2 * dilation_step
        err_three = grad_flow.astype(jnp.bfloat16)
        grad_out = over_tokens(third_activation, err_three)
        grad_bias_out = jnp.sum(err_three.astype(jnp.float32), axis=0)
        flow_three = along_rows(err_three, w_out[index_of_block])
        err_two_full, grad_gain_two, grad_shift_two = third_backward(flow_three)
        err_two = err_two_full.astype(jnp.bfloat16)
        grad_bias_mid = jnp.sum(err_two.astype(jnp.float32), axis=0)
        masked_errs = [
            err_two * tap_masks[tap_index][:, None].astype(jnp.bfloat16)
            for tap_index in range(tap_count)
        ]
        grad_mid = jnp.stack(
            [
                over_tokens(
                    padded[tap_index * dilation_step : tap_index * dilation_step + tok_rows],
                    masked_errs[tap_index],
                )
                for tap_index in range(tap_count)
            ]
        )
        spread = jnp.zeros((tok_rows + 2 * rim_width, padded.shape[1]), jnp.float32)
        for tap_index in range(tap_count):
            spread = spread.at[
                tap_index * dilation_step : tap_index * dilation_step + tok_rows
            ].add(along_rows(masked_errs[tap_index], w_mid[index_of_block, tap_index]))
        rim_below = spread[:rim_width]
        rim_above = spread[tok_rows + rim_width :]
        if index_of_block == 0:
            from_next = from_behind(rim_below, "seq", -1)
            from_previous = from_behind(rim_above, "seq", 1)
        else:
            from_next = from_behind(rim_below.astype(jnp.bfloat16), "seq", -1).astype(
                rim_below.dtype
            )
            from_previous = from_behind(rim_above.astype(jnp.bfloat16), "seq", 1).astype(
                rim_above.dtype
            )
        flow_two = spread[rim_width : rim_width + tok_rows]
        flow_two = flow_two.at[:rim_width].add(from_previous)
        flow_two = flow_two.at[tok_rows - rim_width :].add(from_next)
        err_one_full, grad_gain_one, grad_shift_one = back_two(flow_two)
        err_one = err_one_full.astype(jnp.bfloat16)
        grad_bias_in = jnp.sum(err_one.astype(jnp.float32), axis=0)
        grad_in = over_tokens(act_one, err_one)
        flow_one = along_rows(err_one, w_in[index_of_block])
        grad_input, grad_gain_first, grad_shift_first = back_one(flow_one)
        grad_flow = grad_flow + grad_input
        shares = (
            lax.psum_scatter(grad_in, "seq", scatter_dimension=0, tiled=True),
            lax.psum_scatter(grad_mid, "seq", scatter_dimension=2, tiled=True),
            lax.psum_scatter(grad_out, "seq", scatter_dimension=1, tiled=True),
        )
        shares = (
            lax.psum(shares[0].astype(jnp.bfloat16), "dp").astype(jnp.float32),
            lax.psum(shares[1].astype(jnp.bfloat16), "dp").astype(jnp.float32),
            lax.psum(shares[2].astype(jnp.bfloat16), "dp").astype(jnp.float32),
        )
        weight_sums[index_of_block] = shares
        vector_sums[index_of_block] = (
            grad_gain_first,
            grad_shift_first,
            jnp.stack([grad_gain_one, grad_gain_two]),
            jnp.stack([grad_shift_one, grad_shift_two]),
            jnp.stack([grad_bias_in, grad_bias_mid]),
            grad_bias_out,
        )
    totals = lax.psum(
        (
            jnp.stack([vector_sums[0][0], vector_sums[1][0]]),
            jnp.stack([vector_sums[0][1], vector_sums[1][1]]),
            jnp.stack([vector_sums[0][2], vector_sums[1][2]]),
            jnp.stack([vector_sums[0][3], vector_sums[1][3]]),
            jnp.stack([vector_sums[0][4], vector_sums[1][4]]),
            jnp.stack([vector_sums[0][5], vector_sums[1][5]]),
        ),
        ("dp", "seq"),
    )
    grad_w_in = jnp.stack([weight_sums[0][0], weight_sums[1][0]])
    grad_w_mid = jnp.stack([weight_sums[0][1], weight_sums[1][1]])
    grad_w_out = jnp.stack([weight_sums[0][2], weight_sums[1][2]])
    return (
        current[None],
        grad_flow[None],
        grad_w_in,
        grad_w_mid,
        grad_w_out,
        totals[0],
        totals[1],
        totals[2],
        totals[3],
        totals[4],
        totals[5],
    )


def solution(mesh):
    placed = (
        P("dp", "seq", None),
        P(None, "dp", "seq"),
        P(),
        P(),
        P(),
        P(),
        P(),
        P(),
        P(),
        P(),
        P(),
        P("dp", "seq", None),
    )
    return jax.shard_map(
        body,
        mesh=mesh,
        in_specs=placed,
        out_specs=(
            P("dp", "seq", None),
            P("dp", "seq", None),
            P(None, "seq", None),
            P(None, None, None, "seq"),
            P(None, None, "seq"),
            P(),
            P(),
            P(),
            P(),
            P(),
            P(),
        ),
        check_vma=False,
    )
```

profile of v0, /device:TPU:0, one launch (start us, length us, event | category | flops | bytes accessed | tf_op | source)
XLA Modules:
  0.0 793.0 jit_solution(3478294447599761259)
XLA Ops:
  9.7 8.4 %fusion.337 = (f32[512]{0:T(512)S(1)}, f32[512,640]{1,0:T(8,128)S(1)}) fusion(f32[640]{0:T(1024)S(1)} %get-tuple-element.231, bf16[2,1280,640]{2,1,0:T(8,128)(2,1)} %param.42, bf16[1,512,1280]{2,1,0:T(8,128)(2,1)S(1)} %copy-done, f32[1280]{0:T(1024)S(1)} %get-tuple-element.237, f32[1280]{0:T(1024)S(1)} %get-tuple-element.235, f32[512]{0:T(512)S(1)} %fusion.263, ...), kind=kOutput, calls=%fused_computation.540 | convolution fusion | flops 885390848 | bytes 4278784 | tf_op jit(solution)/shard_map/dot_general | solution.py:86
  18.4 4.4 multiply_convert_fusion.6
  24.1 6.0 collective-permute-start
  30.3 2.0 convolution_multiply_fusion.7
  34.3 2.1 fusion.86
  39.5 4.4 multiply_convert_fusion.5
  45.7 13.8 %multiply_convert_fusion.1 = (bf16[512,1280]{1,0:T(8,128)(2,1)S(1)}, f32[512,1280]{1,0:T(8,128)}, f32[512,1280]{1,0:T(8,128)}) fusion(f32[512,1280]{1,0:T(8,128)S(1)} %get-tuple-element.309, f32[1280]{0:T(1024)S(1)} %get-tuple-element.236, f32[1280]{0:T(1024)S(1)} %get-tuple-element.234, f32[512]{0:T(512)S(1)} %fusion.266, ...), kind=kLoop, calls=%fused_computation.58 | loop fusion | flops 89128960 | bytes 10514432 | tf_op jit(solution)/shard_map/convert_element_type | solution.py:84
  61.1 4.4 multiply_convert_fusion.4
  65.6 4.8 collective-permute-start.2
  72.7 11.2 %collective-permute-done.2 = bf16[256,640]{1,0:T(8,128)(2,1)S(1)} collective-permute-done((bf16[256,640]{1,0:T(8,128)(2,1)S(1)}, bf16[256,640]{1,0:T(8,128)(2,1)S(1)}, u32[]{:S(2)}, u32[]{:S(2)}) %collective-permute-start.2) | collective-permute-done | bytes 327712 | tf_op jit(solution)/shard_map/ppermute | solution.py:18
  87.4 4.4 multiply_convert_fusion.3
  92.6 2.9 fusion.101
  95.9 4.6 multiply_reduce_fusion.3
  103.4 2.1 fusion.77
  111.5 4.3 collective-permute-start.4
  117.4 14.1 %collective-permute-done.4 = bf16[256,640]{1,0:T(8,128)(2,1)S(1)} collective-permute-done((bf16[256,640]{1,0:T(8,128)(2,1)S(1)}, bf16[256,640]{1,0:T(8,128)(2,1)S(1)}, u32[]{:S(2)}, u32[]{:S(2)}) %collective-permute-start.4) | collective-permute-done | bytes 327712 | tf_op jit(solution)/shard_map/ppermute | solution.py:27
  135.1 2.9 fusion.342
  138.5 5.1 multiply_reduce_fusion
  146.9 3.0 fusion.343
  150.0 4.6 multiply_reduce_fusion.5
  155.4 2.2 fusion.188
  158.8 3.0 convolution_add_fusion.5
  161.8 4.4 scatter-add.60
  166.3 3.7 fusion.74
  169.9 3.5 convolution_add_fusion.3
  173.4 4.4 scatter-add.64
  177.8 2.7 convolution_add_fusion.2
  180.5 5.7 collective-permute-start.6
  189.1 6.6 collective-permute-done.7
  199.5 3.3 fusion.98
  202.9 3.1 bitcast_dynamic-update-slice_fusion.4
  213.7 13.5 %copy.27 = f32[5,640,640]{1,0,2:T(8,128)} copy(f32[5,640,640]{2,1,0:T(8,128)} %bitcast_dynamic-update-slice_fusion) | data formatting | bytes 16384000
  227.2 9.9 %copy.30 = f32[80,8,5,640]{3,1,2,0:T(8,128)} copy(f32[80,8,5,640]{3,2,1,0:T(8,128)} %bitcast.255) | data formatting | bytes 16384000
  238.2 3.1 bitcast_dynamic-update-slice_fusion.9
  243.3 2.0 bitcast_dynamic-update-slice_fusion.7
  249.2 13.5 %copy.25 = f32[5,640,640]{1,0,2:T(8,128)} copy(f32[5,640,640]{2,1,0:T(8,128)} %bitcast_dynamic-update-slice_fusion.5) | data formatting | bytes 16384000
  262.6 9.8 %copy.29 = f32[80,8,5,640]{3,1,2,0:T(8,128)} copy(f32[80,8,5,640]{3,2,1,0:T(8,128)} %bitcast.256) | data formatting | bytes 16384000
  273.5 4.3 fusion.7
  278.0 4.0 fusion.319
  284.2 2.5 convert_reduce_fusion.1
  290.1 48.4 %reduce-scatter.15.cloned.1.call-done = f32[640,160]{0,1:T(8,128)} async-done(((f32[640,1280]{0,1:T(8,128)}), f32[640,160]{0,1:T(8,128)}) %reduce-scatter.15.cloned.1.call-update) | async-done | bytes 409616 | tf_op jit(solution)/shard_map/reduce_scatter | solution.py:174
  340.2 77.3 %reduce-scatter.11.cloned.1.call-done = f32[160,640]{1,0:T(8,128)} async-done(((f32[1280,640]{1,0:T(8,128)}), f32[160,640]{1,0:T(8,128)}) %reduce-scatter.11.cloned.1.call-update) | async-done | bytes 409616 | tf_op jit(solution)/shard_map/reduce_scatter | solution.py:172
  419.2 147.1 %reduce-scatter.21.cloned.1.call-done = f32[80,3200]{1,0:T(8,128)} async-done(((f32[640,3200]{1,0:T(8,128)}), f32[80,3200]{1,0:T(8,128)}) %reduce-scatter.21.cloned.1.call-update) | async-done | bytes 1024016
  569.5 145.7 %reduce-scatter.19.cloned.1.call-done = f32[80,3200]{1,0:T(8,128)} async-done(((f32[640,3200]{1,0:T(8,128)}), f32[80,3200]{1,0:T(8,128)}) %reduce-scatter.19.cloned.1.call-update) | async-done | bytes 1024016
  718.6 41.5 %all-reduce.2 = (f32[2,1280]{1,0:T(2,128)}, f32[2,1280]{1,0:T(2,128)}, f32[2,2,640]{2,1,0:T(2,128)}, f32[2,2,640]{2,1,0:T(2,128)}, f32[2,2,640]{2,1,0:T(2,128)}, /*index=5*/f32[2,1280]{1,0:T(2,128)}) all-reduce(f32[2,1280]{1,0:T(2,128)S(1)} %pad_maximum_fusion.12, ...), channel_id=1, replica_groups=mesh['dp'=4,'seq'=8] {'dp','seq'}, use_global_device_ids=true, to_apply=%region_38.0 | all-reduce | flops 15360 | bytes 122880 | tf_op jit(solution)/shard_map/psum | solution.py:190
  760.1 16.6 %all-reduce.6.cloned.1.call-done = (bf16[1,160,640]{2,1,0:T(8,128)(2,1)}, bf16[1,160,640]{2,1,0:T(8,128)(2,1)}, bf16[1,5,640,80]{3,2,1,0:T(8,128)(2,1)}, bf16[1,...) async-done(((bf16[1,160,640]{2,1,0:T(8,128)(2,1)}, bf16[1,160,640]{2,1,0:T(8,128)(2,1)}, bf16[1,5,640,80]{3,2,1,0:T(8,128)(2,1)}, ...) | async-done | bytes 1843216 | tf_op jit(solution)/shard_map/psum | solution.py:177
  776.7 3.5 maximum_convert_fusion
  780.2 3.4 copy.24
  (285 shorter events, 79.2 us)
Async XLA Ops:
  7.2 2.4 copy-start.51
  7.2 2.4 copy-start.52
  7.2 279.4 %reduce-scatter.17.cloned.1.call-start = ((), (), s32[]{:S(2)}) async-start(), calls=%async_computation.9 | async-start | bytes 3686400 | tf_op jit(solution)/shard_map/reduce_scatter | solution.py:174
  18.1 4.7 copy-start.9
  18.4 11.7 %copy-start.54 = (s32[2,1,512]{2,1,0:T(1,128)S(1)}, s32[2,1,512]{2,1,0:T(1,128)}, u32[]{:S(2)}) copy-start(s32[2,1,512]{2,1,0:T(1,128)} %param.41) | copy-start | bytes 12292
  18.4 13.9 %copy-start.53 = (f32[2,1280]{1,0:T(2,128)S(1)}, f32[2,1280]{1,0:T(2,128)}, u32[]{:S(2)}) copy-start(f32[2,1280]{1,0:T(2,128)} %param.50) | copy-start | bytes 30724
  22.8 15.5 %copy-start.27 = (bf16[512,640]{1,0:T(8,128)(2,1)}, bf16[512,640]{1,0:T(8,128)(2,1)S(1)}, u32[]{:S(2)}) copy-start(bf16[512,640]{1,0:T(8,128)(2,1)S(1)} %get-tuple-element.280) | copy-start | bytes 1966084
  22.8 13.5 %collective-permute-start.1 = (bf16[8,640]{1,0:T(8,128)(2,1)S(1)}, bf16[8,640]{1,0:T(8,128)(2,1)S(1)}, u32[]{:S(2)}, u32[]{:S(2)}) collective-permute-start(bf16[8,640]{1,0:T(8,128)(2,1)S(1)} %get-tuple-element.288), channel_id=1, source_target_pairs={{1,0},{2,1},{3,2},{4,3},{5,4},{6,5},{7,6},{9,8},{10,9},{11,10},{12... | collective-permute-start | bytes 30728 | tf_op jit(solution)/shard_map/ppermute | solution.py:19
  24.1 8.2 %collective-permute-start = (bf16[8,640]{1,0:T(8,128)(2,1)S(1)}, bf16[8,640]{1,0:T(8,128)(2,1)S(1)}, u32[]{:S(2)}, u32[]{:S(2)}) collective-permute-start(bf16[8,640]{1,0:T(8,128)(2,1)S(1)} %get-tuple-element.289), channel_id=1, source_target_pairs={{0,1},{1,2},{2,3},{3,4},{4,5},{5,6},{6,7},{8,9},{9,10},{10,11},{11... | collective-permute-start | bytes 30728 | tf_op jit(solution)/shard_map/ppermute | solution.py:18
  30.2 8.1 %slice-start = ((s8[8192000]{0:T(1024)(128)(4,1)}), s8[4194304]{0:T(1024)(128)(4,1)S(1)}, s32[]{:S(2)}) async-start(s8[8192000]{0:T(1024)(128)(4,1)} %bitcast.259), calls=%async_computation.13 | async-start | bytes 8388608
  34.3 4.1 slice-start.1
  39.2 4.7 copy-start.11
  39.2 4.7 copy-start.39
  39.5 4.4 copy-start.1
  45.7 13.8 %copy-start.55 = (bf16[2,1280,640]{2,1,0:T(8,128)(2,1)S(1)}, bf16[2,1280,640]{2,1,0:T(8,128)(2,1)}, u32[]{:S(2)}) copy-start(bf16[2,1280,640]{2,1,0:T(8,128)(2,1)} %param.42) | copy-start | bytes 9830404
  60.8 4.7 copy-start.13
  65.5 20.6 %copy-start.15 = (bf16[512,640]{1,0:T(8,128)(2,1)}, bf16[512,640]{1,0:T(8,128)(2,1)S(1)}, u32[]{:S(2)}) copy-start(bf16[512,640]{1,0:T(8,128)(2,1)S(1)} %get-tuple-element.274) | copy-start | bytes 1966084
  65.6 18.3 %collective-permute-start.2 = (bf16[256,640]{1,0:T(8,128)(2,1)S(1)}, bf16[256,640]{1,0:T(8,128)(2,1)S(1)}, u32[]{:S(2)}, u32[]{:S(2)}) collective-permute-start(bf16[256,640]{1,0:T(8,128)(2,1)S(1)} %get-tuple-element.287), channel_id=1, source_target_pairs={{0,1},{1,2},{2,3},{3,4},{4,5},{5,6},{6,7},{8,9},{9,10},{10,11},{11... | collective-permute-start | bytes 983048 | tf_op jit(solution)/shard_map/ppermute | solution.py:18
  70.4 14.9 %collective-permute-start.3 = (bf16[256,640]{1,0:T(8,128)(2,1)S(1)}, bf16[256,640]{1,0:T(8,128)(2,1)S(1)}, u32[]{:S(2)}, u32[]{:S(2)}) collective-permute-start(bf16[256,640]{1,0:T(8,128)(2,1)S(1)} %get-tuple-element.286), channel_id=1, source_target_pairs={{1,0},{2,1},{3,2},{4,3},{5,4},{6,5},{7,6},{9,8},{10,9},{11,10},{12... | collective-permute-start | bytes 983048 | tf_op jit(solution)/shard_map/ppermute | solution.py:19
  87.0 4.7 copy-start.7
  87.3 5.3 copy-start.17
  95.6 192.9 %reduce-scatter.13.cloned.1.call-start = ((), (), s32[]{:S(2)}) async-start(), calls=%async_computation.7 | async-start | bytes 3686400 | tf_op jit(solution)/shard_map/reduce_scatter | solution.py:172
  95.9 4.6 copy-start.8
  111.5 19.9 %collective-permute-start.4 = (bf16[256,640]{1,0:T(8,128)(2,1)S(1)}, bf16[256,640]{1,0:T(8,128)(2,1)S(1)}, u32[]{:S(2)}, u32[]{:S(2)}) collective-permute-start(bf16[256,640]{1,0:T(8,128)(2,1)S(1)} %slice.805), channel_id=1, source_target_pairs={{0,1},{1,2},{2,3},{3,4},{4,5},{5,6},{6,7},{8,9},{9,10},{10,11},{11... | collective-permute-start | bytes 983048 | tf_op jit(solution)/shard_map/ppermute | solution.py:27
  116.0 15.5 %collective-permute-start.5 = (bf16[256,640]{1,0:T(8,128)(2,1)S(1)}, bf16[256,640]{1,0:T(8,128)(2,1)S(1)}, u32[]{:S(2)}, u32[]{:S(2)}) collective-permute-start(bf16[256,640]{1,0:T(8,128)(2,1)S(1)} %slice.804), channel_id=1, source_target_pairs={{1,0},{2,1},{3,2},{4,3},{5,4},{6,5},{7,6},{9,8},{10,9},{11,10},{12... | collective-permute-start | bytes 983048 | tf_op jit(solution)/shard_map/ppermute | solution.py:27
  117.4 14.3 %copy-start.14 = (f32[512,640]{1,0:T(8,128)S(1)}, f32[512,640]{1,0:T(8,128)}, u32[]{:S(2)}) copy-start(f32[512,640]{1,0:T(8,128)} %copy-done.13) | copy-start | bytes 3932164
  117.4 14.3 %copy-start.30 = (f32[512,640]{1,0:T(8,128)S(1)}, f32[512,640]{1,0:T(8,128)}, u32[]{:S(2)}) copy-start(f32[512,640]{1,0:T(8,128)} %get-tuple-element.275) | copy-start | bytes 3932164
  137.9 200.6 %reduce-scatter.15.cloned.1.call-start = ((), (), s32[]{:S(2)}) async-start(), calls=%async_computation.8 | async-start | bytes 3686400 | tf_op jit(solution)/shard_map/reduce_scatter | solution.py:174
  149.9 267.6 %reduce-scatter.11.cloned.1.call-start = ((), (), s32[]{:S(2)}) async-start(), calls=%async_computation.6 | async-start | bytes 3686400 | tf_op jit(solution)/shard_map/reduce_scatter | solution.py:172
  150.0 4.7 copy-start.12
  155.4 3.4 copy-start.20
  166.3 3.7 copy-start.21
  177.8 8.4 %copy-start.6 = (f32[528,640]{1,0:T(8,128)S(1)}, f32[528,640]{1,0:T(8,128)}, u32[]{:S(2)}) copy-start(f32[528,640]{1,0:T(8,128)} %scatter-add.64) | copy-start | bytes 4055044
  180.5 7.1 collective-permute-start.6
  186.3 9.5 %copy-start.10 = (f32[512,640]{1,0:T(8,128)S(1)}, f32[512,640]{1,0:T(8,128)}, u32[]{:S(2)}) copy-start(f32[512,640]{1,0:T(8,128)} %copy-done.9) | copy-start | bytes 3932164
  186.3 9.5 %copy-start.29 = (f32[512,640]{1,0:T(8,128)S(1)}, f32[512,640]{1,0:T(8,128)}, u32[]{:S(2)}) copy-start(f32[512,640]{1,0:T(8,128)} %get-tuple-element.281) | copy-start | bytes 3932164
  187.6 8.1 %collective-permute-start.7 = (f32[8,640]{1,0:T(8,128)S(1)}, f32[8,640]{1,0:T(8,128)S(1)}, u32[]{:S(2)}, u32[]{:S(2)}) collective-permute-start(f32[8,640]{1,0:T(8,128)S(1)} %get-tuple-element.282), channel_id=1, source_target_pairs={{1,0},{2,1},{3,2},{4,3},{5,4},{6,5},{7,6},{9,8},{10,9},{11,10},{12... | collective-permute-start | bytes 61448 | tf_op jit(solution)/shard_map/ppermute | solution.py:27
  202.8 363.5 %reduce-scatter.21.cloned.1.call-start = ((), (), s32[]{:S(2)}) async-start(), calls=%async_computation.11 | async-start | bytes 9216000
  202.9 3.1 copy-start.16
  202.9 3.1 copy-start.43
  237.1 478.1 %reduce-scatter.19.cloned.1.call-start = ((), (), s32[]{:S(2)}) async-start(), calls=%async_computation.10 | async-start | bytes 9216000
  238.2 3.1 copy-start.28
  272.4 504.2 %all-reduce.6.cloned.1.call-start = ((), (), s32[]{:S(2)}) async-start(), calls=%async_computation.12 | async-start | bytes 4915200 | tf_op jit(solution)/shard_map/psum | solution.py:177
  273.5 4.5 copy-start.3
  273.5 4.5 copy-start.36
  273.5 4.5 copy-start.41
  780.2 3.4 copy-start.46
  780.2 3.4 copy-start.47
  (25 other events, 36.7 us)
Sparse Core Ops, SparseCore 0:
  95.7 85.0 reduce-scatter.16
  184.8 75.0 reduce-scatter.12
  263.4 75.0 reduce-scatter.14
  342.4 75.0 reduce-scatter.10
  421.0 145.2 reduce-scatter.20
  569.9 145.3 reduce-scatter.18
  718.6 58.0 all-reduce.5
where the time goes:
time: 802 us; the launch traced here: 793 us
  waiting for transfers between devices  468 us (58%)
  matrix products  105 us (13%)
  local copies, waits for them, and re-layouts  76.5 us (10%)
  other arithmetic  58.4 us (7%)
  blocking collectives  41.5 us (5%)
  starting transfers between devices  27.4 us (3%)
  between operations  15.7 us (2%)
    unnamed x9, waiting for transfers between devices  293 us
    reduce_scatter x2, waiting for transfers between devices, body(): lax.psum_scatter(grad_in, 'seq', scatter_dimension=0, tiled=True)  77.3 us
    unnamed x125, local copies, waits for them, and re-layouts  65.6 us
    reduce_scatter x2, waiting for transfers between devices, body(): lax.psum_scatter(grad_out, 'seq', scatter_dimension=1, tiled=True)  48.4 us
    dot_general x14, matrix products, along_rows(): lax.dot_general(left, right, (((1,), (1,)), ((), ())), preferred_element_...  43.3 us
    psum x1, blocking collectives, body(): lax.psum((jnp.stack([vector_sums[0][0], vector_sums[1][0]]), jnp.stack([v...  41.5 us
    dot_general x14, matrix products, over_tokens(): lax.dot_general(left, right, (((0,), (0,)), ((), ())), preferred_element_...  33.8 us
    ppermute x4, waiting for transfers between devices, from_behind(): return lax.ppermute(x, axis, pairs)  21.9 us
  transfers between devices with their start and end apart: 15, of which 9 were waited for; matrix products, arithmetic and copies ran while one was open for 21% of the time, Pallas kernels for 0%

commit v1 on v0

v1 whole, which is shorter than its diff:
```python
import functools

import jax
import jax.numpy as jnp
from jax import lax
from jax.experimental import pallas as pl
from jax.experimental.pallas import tpu as pltpu
from jax.sharding import PartitionSpec as P

DILATION_CLOSE = 4
DILATION_BROAD = 128
EPS = 1e-05
F32 = jnp.float32
BF16 = jnp.bfloat16
VMEM_LIMIT = 56 * 1024 * 1024

C0 = 0.3275911 * 0.7071067811865476
POLY = tuple(0.5 * c for c in (0.254829592, -0.284496736, 1.421413741, -1.453152027, 1.061405429))
ROOT_2PI = 0.3989422804014327


def normal_parts(q):
    bell = jnp.exp(-0.5 * q * q)
    den = 1.0 + C0 * jnp.abs(q)
    t = pl.reciprocal(den, approx=True)
    t = t * (2.0 - den * t)
    h = POLY[4]
    for c in POLY[3::-1]:
        h = h * t + c
    tail = h * t * bell
    return jnp.where(q >= 0, 1.0 - tail, tail), q * bell * ROOT_2PI


def act_forward(v, gain, shift):
    c = v.shape[-1]
    centred = v - jnp.sum(v, axis=-1, keepdims=True) * (1.0 / c)
    r = lax.rsqrt(jnp.sum(centred * centred, axis=-1, keepdims=True) * (1.0 / c) + EPS)
    n = centred * r
    q = n * gain + shift
    below, slope = normal_parts(q)
    return n, r, q * below, below + slope


def act_backward(f, n, r, d, gain):
    c = f.shape[-1]
    p = f * d
    gp = gain * p
    first = jnp.sum(gp, axis=-1, keepdims=True) * (1.0 / c)
    second = jnp.sum(gp * n, axis=-1, keepdims=True) * (1.0 / c)
    return p, r * (gp - first - n * second)


def fold(v):
    return jnp.sum(v.reshape(v.shape[0] // 8, 8, v.shape[1]), axis=0)


def total(acc):
    return jnp.sum(acc, axis=0, keepdims=True)


def strips(rows, height, step, carry=()):
    def body(i, c):
        return step(pl.ds(pl.multiple_of(i * height, height), height), c)

    return lax.fori_loop(0, rows // height, body, carry)


def dot(a, b):
    return jnp.dot(a, b, preferred_element_type=F32)


def dot_nt(a, b):
    return lax.dot_general(a, b, (((1,), (1,)), ((), ())), preferred_element_type=F32)


def dot_tn(a, b):
    return lax.dot_general(a, b, (((0,), (0,)), ((), ())), preferred_element_type=F32)


def call(kernel, outs, args, scratch=(), flops=0, name=None):
    nbytes = sum(a.size * a.dtype.itemsize for a in args)
    out_shape = [jax.ShapeDtypeStruct(s, t) for s, t in outs]
    nbytes += sum(a.size * a.dtype.itemsize for a in out_shape)
    return pl.pallas_call(
        kernel,
        out_shape=out_shape,
        in_specs=[pl.BlockSpec(memory_space=pltpu.VMEM)] * len(args),
        out_specs=[pl.BlockSpec(memory_space=pltpu.VMEM)] * len(outs),
        scratch_shapes=list(scratch),
        compiler_params=pltpu.CompilerParams(vmem_limit_bytes=VMEM_LIMIT),
        cost_estimate=pl.CostEstimate(flops=flops, bytes_accessed=nbytes, transcendentals=0),
        name=name,
    )(*args)


def first_half(x_ref, w_in, vecw, vecn, a1, n1, d1, r1, a2, n2, d2, r2, z):
    rows = x_ref.shape[0]

    def wide(at, c):
        n, r, a, d = act_forward(x_ref[at].astype(F32), vecw[0:1], vecw[1:2])
        n1[at], d1[at], a1[at] = n, d, a.astype(BF16)
        r1[at] = jnp.broadcast_to(r, (r.shape[0], 128))
        return c

    strips(rows, 16, wide)
    z[...] = dot(a1[...], w_in[...]) + vecn[2:3]

    def narrow(at, c):
        n, r, a, d = act_forward(z[at], vecn[0:1], vecn[1:2])
        n2[at], d2[at], a2[at] = n, d, a.astype(BF16)
        r2[at] = jnp.broadcast_to(r, (r.shape[0], 128))
        return c

    strips(rows, 32, narrow)


def windows(before, own, after, masks, win, pad, step):
    rows, width = own.shape
    rim = before.shape[0]
    taps = masks.shape[0]
    pad[0:rim] = before[...].astype(pad.dtype)
    pad[rim : rim + rows] = own[...].astype(pad.dtype)
    pad[rim + rows : rim + rows + rim] = after[...].astype(pad.dtype)
    for k in range(taps):
        start = rim + (k - taps // 2) * step
        for i in range(0, rows, 64):
            m = masks[k, i : i + 64].astype(pad.dtype)
            m = jnp.concatenate([m] * (width // 128), axis=1)
            v = pad[start + i : start + i + 64] * m
            win[i : i + 64, k * width : (k + 1) * width] = v.astype(BF16)


def k_in(x_ref, w_in, vecw, vecn, *rest):
    first_half(x_ref, w_in, vecw, vecn, *rest)


def k_mid(
    x_ref, before, own, after, masks, w_mid, w_out, w_in, vecn, vecw_out, vecw, vecn2,
    win, a3, n3, d3, r3, y, a1, n1, d1, r1, a2, n2, d2, r2, pad, z, *, step,
):
    rows = x_ref.shape[0]
    windows(before, own, after, masks, win, pad, step)
    z[...] = dot(win[...], w_mid[...]) + vecn[2:3]

    def narrow(at, c):
        n, r, a, d = act_forward(z[at], vecn[0:1], vecn[1:2])
        n3[at], d3[at], a3[at] = n, d, a.astype(BF16)
        r3[at] = jnp.broadcast_to(r, (r.shape[0], 128))
        return c

    strips(rows, 32, narrow)
    y[...] = x_ref[...].astype(F32) + dot(a3[...], w_out[...]) + vecw_out[0:1]
    first_half(y, w_in, vecw, vecn2, a1, n1, d1, r1, a2, n2, d2, r2, z)


def k_flow(e, w_out, f, sums):
    f[...] = dot_nt(e[...], w_out[...])

    def step(at, acc):
        return acc + fold(e[at].astype(F32))

    sums[...] = total(strips(e.shape[0], 32, step, jnp.zeros((8, e.shape[1]), F32)))


def k_conv(before, own, after, masks, w_mid, vecn, f, win, a3, e2, sums, pad, z, *, step):
    rows, width = own.shape
    windows(before, own, after, masks, win, pad, step)
    z[...] = dot(win[...], w_mid[...]) + vecn[2:3]

    def narrow(at, c):
        n, r, a, d = act_forward(z[at], vecn[0:1], vecn[1:2])
        a3[at] = a.astype(BF16)
        p, v = act_backward(f[at], n, r, d, vecn[0:1])
        e = v.astype(BF16)
        e2[at] = e
        return c[0] + fold(p * n), c[1] + fold(p), c[2] + fold(e.astype(F32))

    zero = jnp.zeros((8, width), F32)
    for i, acc in enumerate(strips(rows, 32, narrow, (zero,) * 3)):
        sums[i : i + 1] = total(acc)


def k_out(x, a3, w_out, bias, y):
    y[...] = x[...] + dot(a3[...], w_out[...]) + bias[0:1]


def k_weights(*refs, shapes):
    pairs, outs = refs[: 2 * len(shapes)], refs[2 * len(shapes) :]
    for i, taps in enumerate(shapes):
        left, right = pairs[2 * i], pairs[2 * i + 1]
        left_t = left[...].T
        if taps == 1:
            outs[i][...] = dot(left_t, right[...]).astype(BF16)
        else:
            width = right.shape[1] // taps
            for k in range(taps):
                outs[i][k] = dot(left_t, right[:, k * width : (k + 1) * width]).astype(BF16)


def back_narrow(f, n, d, r, gain, e_out, sums):
    rows, width = f.shape

    def step(at, c):
        nn = n[at]
        p, v = act_backward(f[at], nn, r[at][:, 0:1], d[at], gain[0:1])
        e = v.astype(BF16)
        e_out[at] = e
        return c[0] + fold(p * nn), c[1] + fold(p), c[2] + fold(e.astype(F32))

    zero = jnp.zeros((8, width), F32)
    for i, acc in enumerate(strips(rows, 32, step, (zero,) * 3)):
        sums[i : i + 1] = total(acc)


def back_wide(f, n, d, r, gain, dy, dx, sums):
    rows, width = f.shape

    def step(at, c):
        nn = n[at]
        p, v = act_backward(f[at], nn, r[at][:, 0:1], d[at], gain[0:1])
        dx[at] = dy[at].astype(F32) + v
        return c[0] + fold(p * nn), c[1] + fold(p)

    zero = jnp.zeros((8, width), F32)
    for i, acc in enumerate(strips(rows, 16, step, (zero,) * 2)):
        sums[i : i + 1] = total(acc)


def flow_two(win, w_mid, z):
    taps = w_mid.shape[0]
    width = w_mid.shape[1]
    for j in range(taps):
        part = dot_nt(win[:, j * width : (j + 1) * width], w_mid[taps - 1 - j])
        if j == 0:
            z[...] = part
        else:
            z[...] += part


def k_back1(
    before, own, after, masks, w_mid, w_in, n2, d2, r2, vecn, n1, d1, r1, vecw, dy,
    w_out0, n3, d3, r3, vecn0,
    e1, sums1, sums_w, dx, e3, sums_e3, e2, sums2, win, pad, z, f1, *, step,
):
    windows(before, own, after, masks, win, pad, step)
    flow_two(win, w_mid, z)
    back_narrow(z, n2, d2, r2, vecn, e1, sums1)
    f1[...] = dot_nt(e1[...], w_in[...])
    back_wide(f1, n1, d1, r1, vecw, dy, dx, sums_w)

    def cast(at, acc):
        e = dx[at].astype(BF16)
        e3[at] = e
        return acc + fold(e.astype(F32))

    sums_e3[...] = total(strips(dx.shape[0], 32, cast, jnp.zeros((8, dx.shape[1]), F32)))
    z[...] = dot_nt(e3[...], w_out0[...])
    back_narrow(z, n3, d3, r3, vecn0, e2, sums2)


def k_back0(
    before, own, after, masks, w_mid, w_in, n2, d2, r2, vecn, n1, d1, r1, vecw, dy,
    e1, sums1, sums_w, dx, win, pad, z, f1, *, step,
):
    windows(before, own, after, masks, win, pad, step)
    flow_two(win, w_mid, z)
    back_narrow(z, n2, d2, r2, vecn, e1, sums1)
    f1[...] = dot_nt(e1[...], w_in[...])
    back_wide(f1, n1, d1, r1, vecw, dy, dx, sums_w)


def halos(v, rim):
    count = lax.axis_size("seq")
    up = [(i, i + 1) for i in range(count - 1)]
    down = [(i + 1, i) for i in range(count - 1)]
    before = lax.ppermute(v[v.shape[0] - rim :], "seq", up)
    after = lax.ppermute(v[:rim], "seq", down)
    return before, after


def swap(v, axis, bit):
    count = lax.axis_size(axis)
    return lax.ppermute(v, axis, [(i, i ^ (1 << bit)) for i in range(count)])


def my_bit(axis, bit):
    return (lax.axis_index(axis) >> bit) & 1


def bits_of(count):
    return count.bit_length() - 1


def halve(v, axis, bit, dim):
    mine = my_bit(axis, bit)
    send = lax.dynamic_index_in_dim(v, 1 - mine, dim, keepdims=False)
    keep = lax.dynamic_index_in_dim(v, mine, dim, keepdims=False)
    got = swap(send, axis, bit)
    return (keep.astype(F32) + got.astype(F32)).astype(BF16)


def widen(v, axis, bit):
    got = swap(v, axis, bit)
    mine = my_bit(axis, bit) == 0
    return jnp.stack([jnp.where(mine, v, got), jnp.where(mine, got, v)])


def reduce_chunk(v, seq_first):
    shards, units, u, width = v.shape
    n = bits_of(shards)
    v = v.reshape((2,) * n + (units, 2, u // 2, width))
    v = halve(v, "dp", 0, n + 1)
    split = units % 2 == 0 and not seq_first

    def along_seq(v, n):
        for bit in range(n):
            v = halve(v, "seq", bit, n - 1 - bit)
        return v

    if split:
        v = v.reshape((2,) * n + (2, units // 2, u // 2, width))
        v = halve(v, "dp", 1, n)
        v = along_seq(v, n)
        v = widen(v, "dp", 1).reshape(units, u // 2, width)
    else:
        v = along_seq(v, n)
        v = (v.astype(F32) + swap(v, "dp", 1).astype(F32)).astype(BF16)
    v = widen(v, "dp", 0)
    return jnp.moveaxis(v, 0, 1).reshape(units, u, width).astype(F32)


def sum_everywhere(v):
    for axis in ("dp", "seq"):
        for bit in range(bits_of(lax.axis_size(axis))):
            v = v + swap(v, axis, bit)
    return v


def make_masks(bounds, taps, step):
    rows = bounds.shape[2]
    position = lax.axis_index("seq") * rows + jnp.arange(rows, dtype=jnp.int32)
    offsets = (jnp.arange(taps, dtype=jnp.int32) - taps // 2) * step
    target = position[None, :] + offsets[:, None]
    inside = (bounds[0, 0][None, :] <= target) & (target < bounds[1, 0][None, :])
    return jnp.broadcast_to(inside.astype(BF16)[:, :, None], (taps, rows, 128))


def body(
    tokens, bounds, w_in, w_mid, w_out, gain_wide, shift_wide, gain_narrow, shift_narrow,
    bias_narrow, bias_wide, cotangent,
):
    x0 = tokens[0]
    cot = cotangent[0]
    rows, width = x0.shape
    taps, inner = w_mid.shape[1], w_mid.shape[2]
    shards = lax.axis_size("seq")
    u = inner // shards
    steps = (DILATION_CLOSE, DILATION_BROAD)
    masks = [make_masks(bounds, taps, step) for step in steps]
    flat_mid = [w_mid[b].reshape(taps * inner, inner) for b in range(2)]
    vecw = [jnp.stack([gain_wide[b], shift_wide[b]]) for b in range(2)]
    vecn = [
        [jnp.stack([gain_narrow[b, i], shift_narrow[b, i], bias_narrow[b, i]]) for i in range(2)]
        for b in range(2)
    ]
    wide_bias = [bias_wide[b][None] for b in range(2)]

    f_wide, f_narrow = (rows, width), (rows, inner)
    mm = 2 * rows * width * inner
    mid = 2 * rows * taps * inner * inner
    saved_in = [
        (f_wide, BF16), (f_wide, F32), (f_wide, F32), ((rows, 128), F32),
        (f_narrow, BF16), (f_narrow, F32), (f_narrow, F32), ((rows, 128), F32),
    ]
    z_scratch = pltpu.VMEM(f_narrow, F32)
    pads = [
        pltpu.VMEM((rows + 4 * steps[0], inner), F32),
        pltpu.VMEM((rows + 4 * steps[1], inner), BF16),
    ]
    win_shape = (rows, taps * inner)

    a1_0, n1_0, d1_0, r1_0, a2_0, n2_0, d2_0, r2_0 = call(
        k_in, saved_in, (x0, w_in[0], vecw[0], vecn[0][0]), [z_scratch], mm, "k_in"
    )
    before, after = halos(a2_0, 2 * steps[0])
    (
        win_0, a3_0, n3_0, d3_0, r3_0, y0, a1_1, n1_1, d1_1, r1_1, a2_1, n2_1, d2_1, r2_1,
    ) = call(
        functools.partial(k_mid, step=steps[0]),
        [(win_shape, BF16), (f_narrow, BF16), (f_narrow, F32), (f_narrow, F32),
         ((rows, 128), F32), (f_wide, F32)] + saved_in,
        (x0, before, a2_0, after, masks[0], flat_mid[0], w_out[0], w_in[1], vecn[0][1],
         wide_bias[0], vecw[1], vecn[1][0]),
        [pads[0], z_scratch], mid + 2 * mm, "k_mid",
    )
    before, after = halos(a2_1, 2 * steps[1])
    f3_1, sum_e3_1 = call(
        k_flow, [(f_narrow, F32), ((1, width), F32)], (cot, w_out[1]), (), mm, "k_flow"
    )
    win_1, a3_1, e2_1, sums2_1 = call(
        functools.partial(k_conv, step=steps[1]),
        [(win_shape, BF16), (f_narrow, BF16), (f_narrow, BF16), ((3, inner), F32)],
        (before, a2_1, after, masks[1], flat_mid[1], vecn[1][1], f3_1),
        [pads[1], z_scratch], mid, "k_conv",
    )
    before, after = halos(e2_1, 2 * steps[1])
    (y1,) = call(k_out, [(f_wide, F32)], (y0, a3_1, w_out[1], wide_bias[1]), (), mm, "k_out")
    g_out_1, g_mid_1 = call(
        functools.partial(k_weights, shapes=(1, taps)),
        [((width, inner), BF16), ((taps, inner, inner), BF16)],
        (cot, a3_1, e2_1, win_1), (), mm + mid, "k_weights1",
    )
    e1_1, sums1_1, sums_w_1, dx_1, e3_0, sum_e3_0, e2_0, sums2_0 = call(
        functools.partial(k_back1, step=steps[1]),
        [(f_narrow, BF16), ((3, inner), F32), ((2, width), F32), (f_wide, F32), (f_wide, BF16),
         ((1, width), F32), (f_narrow, BF16), ((3, inner), F32)],
        (before, e2_1, after, masks[1], w_mid[1], w_in[1], n2_1, d2_1, r2_1, vecn[1][0],
         n1_1, d1_1, r1_1, vecw[1], cot, w_out[0], n3_0, d3_0, r3_0, vecn[0][1]),
        [pltpu.VMEM(win_shape, BF16), pads[1], z_scratch, pltpu.VMEM(f_wide, F32)],
        mid + 2 * mm, "k_back1",
    )
    before, after = halos(e2_0, 2 * steps[0])
    g_in_1, g_out_0, g_mid_0 = call(
        functools.partial(k_weights, shapes=(1, 1, taps)),
        [((width, inner), BF16), ((width, inner), BF16), ((taps, inner, inner), BF16)],
        (a1_1, e1_1, e3_0, a3_0, e2_0, win_0), (), 2 * mm + mid, "k_weights2",
    )
    e1_0, sums1_0, sums_w_0, dx_0 = call(
        functools.partial(k_back0, step=steps[0]),
        [(f_narrow, BF16), ((3, inner), F32), ((2, width), F32), (f_wide, F32)],
        (before, e2_0, after, masks[0], w_mid[0], w_in[0], n2_0, d2_0, r2_0, vecn[0][0],
         n1_0, d1_0, r1_0, vecw[0], dx_1),
        [pltpu.VMEM(win_shape, BF16), pads[0], z_scratch, pltpu.VMEM(f_wide, F32)],
        mid + mm, "k_back0",
    )
    (g_in_0,) = call(
        functools.partial(k_weights, shapes=(1,)),
        [((width, inner), BF16)], (a1_0, e1_0), (), mm, "k_weights3",
    )

    def pair(v):
        return v.reshape(shards, 2, u, inner)

    def by_shard(v):
        return jnp.swapaxes(v.reshape(v.shape[0], shards, u, inner), 0, 1)

    s_mid_1a = reduce_chunk(by_shard(g_mid_1[:4]), False)
    s_1b = reduce_chunk(jnp.concatenate([pair(g_out_1), by_shard(g_mid_1[4:])], axis=1), True)
    s_mid_0a = reduce_chunk(by_shard(g_mid_0[:4]), False)
    s_2b = reduce_chunk(
        jnp.concatenate([pair(g_out_0), by_shard(g_mid_0[4:]), pair(g_in_1)], axis=1), True
    )
    s_3 = reduce_chunk(pair(g_in_0), False)

    vec = jnp.concatenate(
        [sums2_0, sums2_1, sums1_0, sums1_1,
         sums_w_0.reshape(-1, inner), sums_w_1.reshape(-1, inner),
         sum_e3_0.reshape(-1, inner), sum_e3_1.reshape(-1, inner)]
    )
    vec = sum_everywhere(vec)
    two = width // inner
    s2_0, s2_1, s1_0, s1_1 = vec[0:3], vec[3:6], vec[6:9], vec[9:12]
    wide = vec[12:].reshape(6, two * inner)

    def shard_of(v):
        return v.reshape(-1, inner)

    grad_w_in = jnp.stack([shard_of(s_3), shard_of(s_2b[3:5])])
    grad_w_mid = jnp.stack(
        [jnp.concatenate([s_mid_0a, s_2b[2:3]]), jnp.concatenate([s_mid_1a, s_1b[2:3]])]
    ).swapaxes(2, 3)
    grad_w_out = jnp.stack([shard_of(s_2b[0:2]), shard_of(s_1b[0:2])]).swapaxes(1, 2)
    narrow = [jnp.stack([jnp.stack([s1_0[i], s2_0[i]]), jnp.stack([s1_1[i], s2_1[i]])]) for i in range(3)]
    return (
        y1[None],
        dx_0[None],
        grad_w_in,
        grad_w_mid,
        grad_w_out,
        jnp.stack([wide[0], wide[2]]),
        jnp.stack([wide[1], wide[3]]),
        narrow[0],
        narrow[1],
        narrow[2],
        jnp.stack([wide[4], wide[5]]),
    )


def solution(mesh):
    row = P("dp", "seq", None)
    return jax.shard_map(
        body,
        mesh=mesh,
        in_specs=(row, P(None, "dp", "seq")) + (P(),) * 9 + (row,),
        out_specs=(
            row,
            row,
            P(None, "seq", None),
            P(None, None, None, "seq"),
            P(None, None, "seq"),
        )
        + (P(),) * 6,
        check_vma=False,
    )
```

time: 802 us -> 404 us (0.50)
  waiting for transfers between devices: 468 us -> 122 us
  Pallas kernels: 0 us -> 143 us
  matrix products: 105 us -> 0 us
  blocking collectives: 41.5 us -> 0 us
  starting transfers between devices: 27.4 us -> 63.2 us
  local copies, waits for them, and re-layouts: 76.5 us -> 40.9 us
  other arithmetic: 58.4 us -> 25.3 us
  between operations: 15.7 us -> 2.19 us
    unnamed x9 -> x0, waiting for transfers between devices: 293 us -> none
    pallas_call x0 -> x10, Pallas kernels: none -> 143 us  [call(): pl.pallas_call(kernel, out_shape=out_shape, in_specs=[pl.BlockSpec(memory...]
    reduce_scatter x4 -> x0, waiting for transfers between devices: 126 us -> none  [the longest x2 77.3 us: body(): lax.psum_scatter(grad_in, 'seq', scatter_dimension=0, tiled=True)]
    dot_general x42 -> x0, matrix products: 105 us -> none  [the longest x14 43.3 us: along_rows(): lax.dot_general(left, right, (((1,), (1,)), ((), ())), preferred_element_...]
    ppermute x8 -> x46, waiting for transfers between devices: 33.1 us -> 122 us  [the longest x38 112 us: swap(): return lax.ppermute(v, axis, [(i, i ^ 1 << bit) for i in range(count)])]
    unnamed x125 -> x63, local copies, waits for them, and re-layouts: 65.6 us -> 2.3 us
    psum x1 -> x0, blocking collectives: 41.5 us -> none  [body(): lax.psum((jnp.stack([vector_sums[0][0], vector_sums[1][0]]), jnp.stack([v...]
    ppermute x8 -> x46, starting transfers between devices: 26.3 us -> 63.2 us  [the longest x38 39.1 us: swap(): return lax.ppermute(v, axis, [(i, i ^ 1 << bit) for i in range(count)])]
  transfers between devices with their start and end apart: 15 -> 46, of which waited for: 9 -> 21; matrix products, arithmetic and copies ran while one was open for 21% -> 11% of each run, Pallas kernels for 0% -> 17%
where the time goes in v1:
time: 404 us; the launch traced here: 396 us
  Pallas kernels  143 us (35%)
  waiting for transfers between devices  122 us (30%)
  starting transfers between devices  63.2 us (16%)
  local copies, waits for them, and re-layouts  40.9 us (10%)
  other arithmetic  25.3 us (6%)
    pallas_call x10, Pallas kernels, call(): pl.pallas_call(kernel, out_shape=out_shape, in_specs=[pl.BlockSpec(memory...  143 us
    ppermute x38, waiting for transfers between devices, swap(): return lax.ppermute(v, axis, [(i, i ^ 1 << bit) for i in range(count)])  112 us
    ppermute x38, starting transfers between devices, swap(): return lax.ppermute(v, axis, [(i, i ^ 1 << bit) for i in range(count)])  39.1 us
    ppermute x4, starting transfers between devices, halos(): before = lax.ppermute(v[v.shape[0] - rim:], 'seq', up)  18.4 us
    convert_element_type x23, other arithmetic, halve(): return (keep.astype(F32) + got.astype(F32)).astype(BF16)  9.43 us
    squeeze x1, local copies, waits for them, and re-layouts, body(): w_mid[0]  8.98 us
  transfers between devices with their start and end apart: 46, of which 21 were waited for; matrix products, arithmetic and copies ran while one was open for 11% of the time, Pallas kernels for 17%

profile of v1, /device:TPU:0, one launch (start us, length us, event | category | flops | bytes accessed | tf_op | source)
XLA Modules:
  0.0 396.3 jit_solution(6765572634369639334)
XLA Ops:
  3.0 3.9 slice_bitcast_fusion.1
  8.2 19.8 %k_in.1 = (bf16[512,1280]{1,0:T(8,128)(2,1)}, f32[512,1280]{1,0:T(8,128)}, f32[512,1280]{1,0:T(8,128)}, f32[512,128]{1,0:T(8,128)}, bf16[512,640]{1,0:T(8,128)(2...) custom-call(bf16[512,1280]{1,0:T(8,128)(2,1)} %bitcast.334, ...), custom_call_target="tpu_custom_call" | custom-call | flops 838860800 | bytes 13321728 | tf_op jit(solution)/shard_map/k_in/pallas_call | solution.py:84
  28.7 4.9 %collective-permute-start = (bf16[8,640]{1,0:T(8,128)(2,1)S(1)}, bf16[8,640]{1,0:T(8,128)(2,1)S(1)}, u32[]{:S(2)}, u32[]{:S(2)}) collective-permute-start(bf16[8,640]{1,0:T(8,128)(2,1)S(1)} %get-tuple-element.122), channel_id=1, source_target_pairs={{0,1},{1,2},{2,3},{3,4},{4,5},{5,6},{6,7},{8,9},{9,10},{10,11},{11... | collective-permute-start | bytes 30728 | tf_op jit(solution)/shard_map/ppermute | solution.py:276
  34.9 9.0 %slice_bitcast_fusion.23 = (bf16[5,640,640]{2,1,0:T(8,128)(2,1)}, bf16[5,640,640]{2,1,0:T(8,128)(2,1)}, bf16[1,5,640,640]{3,2,1,0:T(8,128)(2,1)}, bf16[1,5,640,640]{3,2,1,0:T(8,128)(2,1)}) fusion(bf16[2,5,640,640]{3,2,1,0:T(8,128)(2,1)} %param.15), kind=kLoop, calls=%fused_computation.166 | loop fusion | bytes 24576000 | tf_op jit(solution)/shard_map/squeeze | solution.py:431
  43.9 1.9 slice_bitcast_fusion
  49.1 34.6 %k_mid.1 = (bf16[512,3200]{1,0:T(8,128)(2,1)}, bf16[512,640]{1,0:T(8,128)(2,1)}, f32[512,640]{1,0:T(8,128)}, f32[512,640]{1,0:T(8,128)}, f32[512,128]{1,0:T(8,12...) custom-call(bf16[512,1280]{1,0:T(8,128)(2,1)} %bitcast.335, ...), custom_call_target="tpu_custom_call" | custom-call | flops 3774873600 | bytes 29837312 | tf_op jit(solution)/shard_map/k_mid/pallas_call | solution.py:84
  84.8 4.6 %collective-permute-start.2 = (bf16[256,640]{1,0:T(8,128)(2,1)S(1)}, bf16[256,640]{1,0:T(8,128)(2,1)S(1)}, u32[]{:S(2)}, u32[]{:S(2)}) collective-permute-start(bf16[256,640]{1,0:T(8,128)(2,1)S(1)} %get-tuple-element.120), channel_id=1, source_target_pairs={{0,1},{1,2},{2,3},{3,4},{4,5},{5,6},{6,7},{8,9},{9,10},{10,11},{11... | collective-permute-start | bytes 983048 | tf_op jit(solution)/shard_map/ppermute | solution.py:276
  90.8 4.4 %k_flow.1 = (f32[512,640]{1,0:T(8,128)}, f32[1,1280]{1,0:T(1,128)}) custom-call(bf16[512,1280]{1,0:T(8,128)(2,1)} %bitcast.318, bf16[640,1280]{1,0:T(8,128)(2,1)} %get-tuple-element.105.w_out), custom_call_target="tpu_custom_call" | custom-call | flops 838860800 | bytes 4264960 | tf_op jit(solution)/shard_map/k_flow/pallas_call | solution.py:84
  96.6 6.2 %collective-permute-done.2.before = bf16[256,640]{1,0:T(8,128)(2,1)S(1)} collective-permute-done((bf16[256,640]{1,0:T(8,128)(2,1)S(1)}, bf16[256,640]{1,0:T(8,128)(2,1)S(1)}, u32[]{:S(2)}, u32[]{:S(2)}) %collective-permute-start.2) | collective-permute-done | bytes 327712 | tf_op jit(solution)/shard_map/ppermute | solution.py:276
  104.0 13.8 %k_conv.1 = (bf16[512,3200]{1,0:T(8,128)(2,1)}, bf16[512,640]{1,0:T(8,128)(2,1)}, bf16[512,640]{1,0:T(8,128)(2,1)}, f32[3,640]{1,0:T(4,128)}) custom-call(bf16[256,640]{1,0:T(8,128)(2,1)} %copy-done.24, bf16[512,640]{1,0:T(8,128)(2,1)} %get-tuple-element.58.own, bf16[256,640]{1,0:T(8,128)(2,1)} %copy-done.25, bf16[5,512,128]{2,1,0:T(8,128)(2,1)} %broadcast_in_dim.9.masks, ...), custom_call_target="tpu_custom_call" | custom-call | flops 2097152000 | bytes 11975680 | tf_op jit(solution)/shard_map/k_conv/pallas_call | solution.py:84
  119.0 8.6 %k_weights1.1 = (bf16[1280,640]{1,0:T(8,128)(2,1)}, bf16[5,640,640]{2,1,0:T(8,128)(2,1)}) custom-call(bf16[512,1280]{1,0:T(8,128)(2,1)} %bitcast.319, bf16[512,640]{1,0:T(8,128)(2,1)} %get-tuple-element.60.a3.refs_1_, bf16[512,640]{1,0:T(8,128)(2,1)} %get-tuple-element.61.own.refs_2_, bf16[512,3200]{1,0:T(8,128)(2,1)} %get-tuple-element.90.refs_3_), custom_call_target="tpu_custom_call" | custom-call | flops 2936012800 | bytes 11632640 | tf_op jit(solution)/shard_map/k_weights1/pallas_call | solution.py:84
  128.8 2.5 slice.280
  131.3 4.4 %collective-permute-start.4 = (bf16[256,640]{1,0:T(8,128)(2,1)S(1)}, bf16[256,640]{1,0:T(8,128)(2,1)S(1)}, u32[]{:S(2)}, u32[]{:S(2)}) collective-permute-start(bf16[256,640]{1,0:T(8,128)(2,1)S(1)} %get-tuple-element.118), channel_id=1, source_target_pairs={{0,1},{1,2},{2,3},{3,4},{4,5},{5,6},{6,7},{8,9},{9,10},{10,11},{11... | collective-permute-start | bytes 983048 | tf_op jit(solution)/shard_map/ppermute | solution.py:276
  140.3 5.1 %k_out.1 = f32[512,1280]{1,0:T(8,128)} custom-call(f32[512,1280]{1,0:T(8,128)} %get-tuple-element.57.x, bf16[512,640]{1,0:T(8,128)(2,1)} %get-tuple-element.60.a3.refs_1_, bf16[640,1280]{1,0:T(8,128)(2,1)} %get-tuple-element.105.w_out, f32[1,1280]{1,0:T(1,128)} %get-tuple-element.157.bias), custom_call_target="tpu_custom_call" | custom-call | flops 838860800 | bytes 7541760 | tf_op jit(solution)/shard_map/k_out/pallas_call | solution.py:84
  145.4 3.1 collective-permute-done.5.after
  149.3 24.1 %k_back1.1 = (bf16[512,640]{1,0:T(8,128)(2,1)}, f32[3,640]{1,0:T(4,128)}, f32[2,1280]{1,0:T(2,128)}, f32[512,1280]{1,0:T(8,128)}, bf16[512,1280]{1,0:T(8,128)(2,...) custom-call(bf16[256,640]{1,0:T(8,128)(2,1)} %copy-done.11, ...), custom_call_target="tpu_custom_call" | custom-call | flops 3774873600 | bytes 27220992 | tf_op jit(solution)/shard_map/k_back1/pallas_call | solution.py:84
  174.1 4.5 %collective-permute-start.6 = (bf16[8,640]{1,0:T(8,128)(2,1)S(1)}, bf16[8,640]{1,0:T(8,128)(2,1)S(1)}, u32[]{:S(2)}, u32[]{:S(2)}) collective-permute-start(bf16[8,640]{1,0:T(8,128)(2,1)S(1)} %get-tuple-element.116), channel_id=1, source_target_pairs={{0,1},{1,2},{2,3},{3,4},{4,5},{5,6},{6,7},{8,9},{9,10},{10,11},{11... | collective-permute-start | bytes 30728 | tf_op jit(solution)/shard_map/ppermute | solution.py:276
  180.3 10.1 %k_weights2.1 = (bf16[1280,640]{1,0:T(8,128)(2,1)}, bf16[1280,640]{1,0:T(8,128)(2,1)}, bf16[5,640,640]{2,1,0:T(8,128)(2,1)}) custom-call(bf16[512,1280]{1,0:T(8,128)(2,1)} %get-tuple-element.82.refs_0_, bf16[512,640]{1,0:T(8,128)(2,1)} %get-tuple-element.83.refs_1_, bf16[512,1280]{1,0:T(8,128)(2,1)} %get-tuple-element.84.refs_2_, ...), custom_call_target="tpu_custom_call" | custom-call | flops 3774873600 | bytes 15237120 | tf_op jit(solution)/shard_map/k_weights2/pallas_call | solution.py:84
  190.5 2.1 slice.275
  193.2 18.6 %k_back0.1 = (bf16[512,640]{1,0:T(8,128)(2,1)}, f32[3,640]{1,0:T(4,128)}, f32[2,1280]{1,0:T(2,128)}, f32[512,1280]{1,0:T(8,128)}) custom-call(bf16[8,640]{1,0:T(8,128)(2,1)} %copy-done.13, bf16[512,640]{1,0:T(8,128)(2,1)} %get-tuple-element.71.own.refs_4_, bf16[8,640]{1,0:T(8,128)(2,1)} %copy-done.14, bf16[5,512,128]{2,1,0:T(8,128)(2,1)} %broadcast_in_dim.8.masks, ...), custom_call_target="tpu_custom_call" | custom-call | flops 2936012800 | bytes 21388288 | tf_op jit(solution)/shard_map/k_back0/pallas_call | solution.py:84
  213.5 2.7 pad_maximum_fusion
  220.7 6.1 %collective-permute-start.43 = (f32[24,640]{1,0:T(8,128)S(1)}, f32[24,640]{1,0:T(8,128)S(1)}, u32[]{:S(2)}, u32[]{:S(2)}) collective-permute-start(f32[24,640]{1,0:T(8,128)S(1)} %add.274), channel_id=1, source_target_pairs={{0,1},{1,0},{2,3},{3,2},{4,5},{5,4},{6,7},{7,6},{8,9},{9,8},{10,11... | collective-permute-start | bytes 184328 | tf_op jit(solution)/shard_map/ppermute | solution.py:283
  229.0 3.5 collective-permute-start.44
  232.5 3.9 k_weights3.1
  236.4 2.7 collective-permute-start.45
  249.8 8.4 %collective-permute-done.9 = bf16[2,2,2,1,40,640]{5,4,3,2,1,0:T(8,128)(2,1)S(1)} collective-permute-done((bf16[2,2,2,1,40,640]{5,4,3,2,1,0:T(8,128)(2,1)S(1)}, bf16[2,2,2,1,40,640]{5,4,3,2,1,0:T(8,128)(2,1)S(1)}, u32[]{:S(2)}, u32[]{:S(2)}) %collective-permute-start.9) | collective-permute-done | bytes 409632 | tf_op jit(solution)/shard_map/ppermute | solution.py:283
  258.6 1.8 fusion.1
  262.3 7.8 %collective-permute-done.10 = bf16[2,2,1,40,640]{4,3,1,0,2:T(8,128)(2,1)S(1)} collective-permute-done((bf16[2,2,1,40,640]{4,3,1,0,2:T(8,128)(2,1)S(1)}, bf16[2,2,1,40,640]{4,3,1,0,2:T(8,128)(2,1)S(1)}, u32[]{:S(2)}, u32[]{:S(2)}) %collective-permute-start.10) | collective-permute-done | bytes 204832 | tf_op jit(solution)/shard_map/ppermute | solution.py:283
  270.4 4.5 %collective-permute-done.11 = bf16[2,1,40,640]{3,2,0,1:T(8,128)(2,1)S(1)} collective-permute-done((bf16[2,1,40,640]{3,2,0,1:T(8,128)(2,1)S(1)}, bf16[2,1,40,640]{3,2,0,1:T(8,128)(2,1)S(1)}, u32[]{:S(2)}, u32[]{:S(2)}) %collective-permute-start.11) | collective-permute-done | bytes 102432 | tf_op jit(solution)/shard_map/ppermute | solution.py:283
  274.9 2.2 collective-permute-start.12
  277.7 2.6 collective-permute-done.12
  282.0 1.9 fusion.2
  287.4 6.2 %collective-permute-done.38 = bf16[3,40,640]{2,1,0:T(8,128)(2,1)S(1)} collective-permute-done((bf16[3,40,640]{2,1,0:T(8,128)(2,1)S(1)}, bf16[3,40,640]{2,1,0:T(8,128)(2,1)S(1)}, u32[]{:S(2)}, u32[]{:S(2)}) %collective-permute-start.38) | collective-permute-done | bytes 153632 | tf_op jit(solution)/shard_map/ppermute | solution.py:283
  293.6 2.0 collective-permute-start.39
  295.7 9.7 %collective-permute-done.39 = bf16[3,40,640]{2,1,0:T(8,128)(2,1)S(1)} collective-permute-done((bf16[3,40,640]{2,1,0:T(8,128)(2,1)S(1)}, bf16[3,40,640]{2,1,0:T(8,128)(2,1)S(1)}, u32[]{:S(2)}, u32[]{:S(2)}) %collective-permute-start.39) | collective-permute-done | bytes 153632 | tf_op jit(solution)/shard_map/ppermute | solution.py:283
  306.1 2.1 fusion
  308.3 1.8 collective-permute-start.16
  310.2 7.9 %collective-permute-done.30 = bf16[2,2,2,40,640]{4,3,2,0,1:T(8,128)(2,1)S(1)} collective-permute-done((bf16[2,2,2,40,640]{4,3,2,0,1:T(8,128)(2,1)S(1)}, bf16[2,2,2,40,640]{4,3,2,0,1:T(8,128)(2,1)S(1)}, u32[]{:S(2)}, u32[]{:S(2)}) %collective-permute-start.30) | collective-permute-done | bytes 409632 | tf_op jit(solution)/shard_map/ppermute | solution.py:283
  319.1 5.5 %collective-permute-done.31 = bf16[2,2,40,640]{3,2,1,0:T(8,128)(2,1)S(1)} collective-permute-done((bf16[2,2,40,640]{3,2,1,0:T(8,128)(2,1)S(1)}, bf16[2,2,40,640]{3,2,1,0:T(8,128)(2,1)S(1)}, u32[]{:S(2)}, u32[]{:S(2)}) %collective-permute-start.31) | collective-permute-done | bytes 204832 | tf_op jit(solution)/shard_map/ppermute | solution.py:283
  324.7 2.1 collective-permute-start.32
  326.9 4.2 %collective-permute-done.32 = bf16[2,40,640]{2,1,0:T(8,128)(2,1)S(1)} collective-permute-done((bf16[2,40,640]{2,1,0:T(8,128)(2,1)S(1)}, bf16[2,40,640]{2,1,0:T(8,128)(2,1)S(1)}, u32[]{:S(2)}, u32[]{:S(2)}) %collective-permute-start.32) | collective-permute-done | bytes 102432 | tf_op jit(solution)/shard_map/ppermute | solution.py:283
  331.8 16.6 %collective-permute-done.23 = bf16[2,2,2,40,640]{4,3,2,0,1:T(8,128)(2,1)S(1)} collective-permute-done((bf16[2,2,2,40,640]{4,3,2,0,1:T(8,128)(2,1)S(1)}, bf16[2,2,2,40,640]{4,3,2,0,1:T(8,128)(2,1)S(1)}, u32[]{:S(2)}, u32[]{:S(2)}) %collective-permute-start.23) | collective-permute-done | bytes 409632 | tf_op jit(solution)/shard_map/ppermute | solution.py:283
  349.3 2.0 collective-permute-start.17
  351.2 5.4 %collective-permute-done.24 = bf16[2,2,40,640]{3,2,1,0:T(8,128)(2,1)S(1)} collective-permute-done((bf16[2,2,40,640]{3,2,1,0:T(8,128)(2,1)S(1)}, bf16[2,2,40,640]{3,2,1,0:T(8,128)(2,1)S(1)}, u32[]{:S(2)}, u32[]{:S(2)}) %collective-permute-start.24) | collective-permute-done | bytes 204832 | tf_op jit(solution)/shard_map/ppermute | solution.py:283
  356.7 2.1 collective-permute-start.25
  358.9 9.6 %collective-permute-done.17 = bf16[2,5,40,640]{3,2,1,0:T(8,128)(2,1)S(1)} collective-permute-done((bf16[2,5,40,640]{3,2,1,0:T(8,128)(2,1)S(1)}, bf16[2,5,40,640]{3,2,1,0:T(8,128)(2,1)S(1)}, u32[]{:S(2)}, u32[]{:S(2)}) %collective-permute-start.17) | collective-permute-done | bytes 512032 | tf_op jit(solution)/shard_map/ppermute | solution.py:283
  370.2 11.0 %collective-permute-done.18 = bf16[5,40,640]{2,1,0:T(8,128)(2,1)S(1)} collective-permute-done((bf16[5,40,640]{2,1,0:T(8,128)(2,1)S(1)}, bf16[5,40,640]{2,1,0:T(8,128)(2,1)S(1)}, u32[]{:S(2)}, u32[]{:S(2)}) %collective-permute-start.18) | collective-permute-done | bytes 256032 | tf_op jit(solution)/shard_map/ppermute | solution.py:283
  382.0 7.4 %collective-permute-done.19 = bf16[5,40,640]{2,1,0:T(8,128)(2,1)S(1)} collective-permute-done((bf16[5,40,640]{2,1,0:T(8,128)(2,1)S(1)}, bf16[5,40,640]{2,1,0:T(8,128)(2,1)S(1)}, u32[]{:S(2)}, u32[]{:S(2)}) %collective-permute-start.19) | collective-permute-done | bytes 256032 | tf_op jit(solution)/shard_map/ppermute | solution.py:283
  (252 shorter events, 64.2 us)
Async XLA Ops:
  7.0 27.9 %copy-start.23 = (s32[2,1,512]{2,1,0:T(1,128)S(1)}, s32[2,1,512]{2,1,0:T(1,128)}, u32[]{:S(2)}) copy-start(s32[2,1,512]{2,1,0:T(1,128)} %param.13) | copy-start | bytes 12292
  28.7 19.1 %collective-permute-start = (bf16[8,640]{1,0:T(8,128)(2,1)S(1)}, bf16[8,640]{1,0:T(8,128)(2,1)S(1)}, u32[]{:S(2)}, u32[]{:S(2)}) collective-permute-start(bf16[8,640]{1,0:T(8,128)(2,1)S(1)} %get-tuple-element.122), channel_id=1, source_target_pairs={{0,1},{1,2},{2,3},{3,4},{4,5},{5,6},{6,7},{8,9},{9,10},{10,11},{11... | collective-permute-start | bytes 30728 | tf_op jit(solution)/shard_map/ppermute | solution.py:276
  33.6 14.2 %collective-permute-start.1 = (bf16[8,640]{1,0:T(8,128)(2,1)S(1)}, bf16[8,640]{1,0:T(8,128)(2,1)S(1)}, u32[]{:S(2)}, u32[]{:S(2)}) collective-permute-start(bf16[8,640]{1,0:T(8,128)(2,1)S(1)} %get-tuple-element.121), channel_id=1, source_target_pairs={{1,0},{2,1},{3,2},{4,3},{5,4},{6,5},{7,6},{9,8},{10,9},{11,10},{12... | collective-permute-start | bytes 30728 | tf_op jit(solution)/shard_map/ppermute | solution.py:277
  84.8 18.0 %collective-permute-start.2 = (bf16[256,640]{1,0:T(8,128)(2,1)S(1)}, bf16[256,640]{1,0:T(8,128)(2,1)S(1)}, u32[]{:S(2)}, u32[]{:S(2)}) collective-permute-start(bf16[256,640]{1,0:T(8,128)(2,1)S(1)} %get-tuple-element.120), channel_id=1, source_target_pairs={{0,1},{1,2},{2,3},{3,4},{4,5},{5,6},{6,7},{8,9},{9,10},{10,11},{11... | collective-permute-start | bytes 983048 | tf_op jit(solution)/shard_map/ppermute | solution.py:276
  89.3 13.4 %collective-permute-start.3 = (bf16[256,640]{1,0:T(8,128)(2,1)S(1)}, bf16[256,640]{1,0:T(8,128)(2,1)S(1)}, u32[]{:S(2)}, u32[]{:S(2)}) collective-permute-start(bf16[256,640]{1,0:T(8,128)(2,1)S(1)} %get-tuple-element.119), channel_id=1, source_target_pairs={{1,0},{2,1},{3,2},{4,3},{5,4},{6,5},{7,6},{9,8},{10,9},{11,10},{12... | collective-permute-start | bytes 983048 | tf_op jit(solution)/shard_map/ppermute | solution.py:277
  131.3 14.1 %collective-permute-start.4 = (bf16[256,640]{1,0:T(8,128)(2,1)S(1)}, bf16[256,640]{1,0:T(8,128)(2,1)S(1)}, u32[]{:S(2)}, u32[]{:S(2)}) collective-permute-start(bf16[256,640]{1,0:T(8,128)(2,1)S(1)} %get-tuple-element.118), channel_id=1, source_target_pairs={{0,1},{1,2},{2,3},{3,4},{4,5},{5,6},{6,7},{8,9},{9,10},{10,11},{11... | collective-permute-start | bytes 983048 | tf_op jit(solution)/shard_map/ppermute | solution.py:276
  135.7 12.8 %collective-permute-start.5 = (bf16[256,640]{1,0:T(8,128)(2,1)S(1)}, bf16[256,640]{1,0:T(8,128)(2,1)S(1)}, u32[]{:S(2)}, u32[]{:S(2)}) collective-permute-start(bf16[256,640]{1,0:T(8,128)(2,1)S(1)} %get-tuple-element.117), channel_id=1, source_target_pairs={{1,0},{2,1},{3,2},{4,3},{5,4},{6,5},{7,6},{9,8},{10,9},{11,10},{12... | collective-permute-start | bytes 983048 | tf_op jit(solution)/shard_map/ppermute | solution.py:277
  138.5 109.3 %collective-permute-start.35 = (bf16[2,2,2,3,40,640]{5,4,3,2,1,0:T(8,128)(2,1)}, bf16[2,2,2,3,40,640]{5,4,3,2,1,0:T(8,128)(2,1)}, u32[]{:S(2)}, u32[]{:S(2)}) collective-permute-start(bf16[2,2,2,3,40,640]{5,4,3,2,1,0:T(8,128)(2,1)} %fusion.9), channel_id=1, source_target_pairs={{0,8},{8,0},{16,24},{24,16},{1,9},{9,1},{17,25},{25,17},{2,10},{10... | collective-permute-start | bytes 3686408 | tf_op jit(solution)/shard_map/ppermute | solution.py:283
  139.8 118.8 %collective-permute-start.28 = (bf16[2,2,2,4,40,640]{5,4,2,1,0,3:T(8,128)(2,1)}, bf16[2,2,2,4,40,640]{5,4,2,1,0,3:T(8,128)(2,1)}, u32[]{:S(2)}, u32[]{:S(2)}) collective-permute-start(bf16[2,2,2,4,40,640]{5,4,2,1,0,3:T(8,128)(2,1)} %dynamic-slice_bitcast_fusion.1), channel_id=1, source_target_pairs={{0,8},{8,0},{16,24},{24,16},{1,9},{9,1},{17,25},{25,17},{2,10},{10... | collective-permute-start | bytes 4915208 | tf_op jit(solution)/shard_map/ppermute | solution.py:283
  174.1 18.4 %collective-permute-start.6 = (bf16[8,640]{1,0:T(8,128)(2,1)S(1)}, bf16[8,640]{1,0:T(8,128)(2,1)S(1)}, u32[]{:S(2)}, u32[]{:S(2)}) collective-permute-start(bf16[8,640]{1,0:T(8,128)(2,1)S(1)} %get-tuple-element.116), channel_id=1, source_target_pairs={{0,1},{1,2},{2,3},{3,4},{4,5},{5,6},{6,7},{8,9},{9,10},{10,11},{11... | collective-permute-start | bytes 30728 | tf_op jit(solution)/shard_map/ppermute | solution.py:276
  178.7 13.9 %collective-permute-start.7 = (bf16[8,640]{1,0:T(8,128)(2,1)S(1)}, bf16[8,640]{1,0:T(8,128)(2,1)S(1)}, u32[]{:S(2)}, u32[]{:S(2)}) collective-permute-start(bf16[8,640]{1,0:T(8,128)(2,1)S(1)} %get-tuple-element.115), channel_id=1, source_target_pairs={{1,0},{2,1},{3,2},{4,3},{5,4},{6,5},{7,6},{9,8},{10,9},{11,10},{12... | collective-permute-start | bytes 30728 | tf_op jit(solution)/shard_map/ppermute | solution.py:277
  213.4 2.8 collective-permute-start.41
  216.2 4.5 %collective-permute-start.42 = (f32[24,640]{1,0:T(8,128)S(1)}, f32[24,640]{1,0:T(8,128)S(1)}, u32[]{:S(2)}, u32[]{:S(2)}) collective-permute-start(f32[24,640]{1,0:T(8,128)S(1)} %add.273), channel_id=1, source_target_pairs={{0,16},{8,24},{16,0},{24,8},{1,17},{9,25},{17,1},{25,9},{2,18},{10... | collective-permute-start | bytes 184328 | tf_op jit(solution)/shard_map/ppermute | solution.py:283
  219.6 86.6 %collective-permute-start.15 = (bf16[2,2,2,5,40,640]{5,4,3,2,1,0:T(8,128)(2,1)}, bf16[2,2,2,5,40,640]{5,4,3,2,1,0:T(8,128)(2,1)}, u32[]{:S(2)}, u32[]{:S(2)}) collective-permute-start(bf16[2,2,2,5,40,640]{5,4,3,2,1,0:T(8,128)(2,1)} %dynamic-slice_bitcast_fusion), channel_id=1, source_target_pairs={{0,8},{8,0},{16,24},{24,16},{1,9},{9,1},{17,25},{25,17},{2,10},{10... | collective-permute-start | bytes 6144008 | tf_op jit(solution)/shard_map/ppermute | solution.py:283
  220.7 8.3 %collective-permute-start.43 = (f32[24,640]{1,0:T(8,128)S(1)}, f32[24,640]{1,0:T(8,128)S(1)}, u32[]{:S(2)}, u32[]{:S(2)}) collective-permute-start(f32[24,640]{1,0:T(8,128)S(1)} %add.274), channel_id=1, source_target_pairs={{0,1},{1,0},{2,3},{3,2},{4,5},{5,4},{6,7},{7,6},{8,9},{9,8},{10,11... | collective-permute-start | bytes 184328 | tf_op jit(solution)/shard_map/ppermute | solution.py:283
  228.1 53.8 %collective-permute-start.21 = (bf16[2,2,2,4,40,640]{5,4,2,1,0,3:T(8,128)(2,1)}, bf16[2,2,2,4,40,640]{5,4,2,1,0,3:T(8,128)(2,1)}, u32[]{:S(2)}, u32[]{:S(2)}) collective-permute-start(bf16[2,2,2,4,40,640]{5,4,2,1,0,3:T(8,128)(2,1)} %dynamic-slice_bitcast_fusion.2), channel_id=1, source_target_pairs={{0,8},{8,0},{16,24},{24,16},{1,9},{9,1},{17,25},{25,17},{2,10},{10... | collective-permute-start | bytes 4915208 | tf_op jit(solution)/shard_map/ppermute | solution.py:283
  229.0 7.4 %collective-permute-start.44 = (f32[24,640]{1,0:T(8,128)S(1)}, f32[24,640]{1,0:T(8,128)S(1)}, u32[]{:S(2)}, u32[]{:S(2)}) collective-permute-start(f32[24,640]{1,0:T(8,128)S(1)} %add.275), channel_id=1, source_target_pairs={{0,2},{1,3},{2,0},{3,1},{4,6},{5,7},{6,4},{7,5},{8,10},{9,11},{10,... | collective-permute-start | bytes 184328 | tf_op jit(solution)/shard_map/ppermute | solution.py:283
  236.4 5.6 %collective-permute-start.45 = (f32[24,640]{1,0:T(8,128)S(1)}, f32[24,640]{1,0:T(8,128)S(1)}, u32[]{:S(2)}, u32[]{:S(2)}) collective-permute-start(f32[24,640]{1,0:T(8,128)S(1)} %add.276), channel_id=1, source_target_pairs={{0,4},{1,5},{2,6},{3,7},{4,0},{5,1},{6,2},{7,3},{8,12},{9,13},{10,... | collective-permute-start | bytes 184328 | tf_op jit(solution)/shard_map/ppermute | solution.py:283
  242.0 3.9 collective-permute-start.8
  246.2 11.9 %collective-permute-start.9 = (bf16[2,2,2,1,40,640]{5,4,3,2,1,0:T(8,128)(2,1)S(1)}, bf16[2,2,2,1,40,640]{5,4,3,2,1,0:T(8,128)(2,1)S(1)}, u32[]{:S(2)}, u32[]{:S(2)}) collective-permute-start(bf16[2,2,2,1,40,640]{5,4,3,2,1,0:T(8,128)(2,1)S(1)} %constant_dynamic-slice_fusion.4), channel_id=1, source_target_pairs={{0,16},{8,24},{16,0},{24,8},{1,17},{9,25},{17,1},{25,9},{2,18},{10... | collective-permute-start | bytes 1228808 | tf_op jit(solution)/shard_map/ppermute | solution.py:283
  249.5 20.7 %collective-permute-start.36 = (bf16[2,2,3,40,640]{4,3,2,1,0:T(8,128)(2,1)S(1)}, bf16[2,2,3,40,640]{4,3,2,1,0:T(8,128)(2,1)S(1)}, u32[]{:S(2)}, u32[]{:S(2)}) collective-permute-start(bf16[2,2,3,40,640]{4,3,2,1,0:T(8,128)(2,1)S(1)} %dynamic-slice_bitcast_fusion.5), channel_id=1, source_target_pairs={{0,1},{1,0},{2,3},{3,2},{4,5},{5,4},{6,7},{7,6},{8,9},{9,8},{10,11... | collective-permute-start | bytes 1843208 | tf_op jit(solution)/shard_map/ppermute | solution.py:283
  258.3 11.7 %collective-permute-start.10 = (bf16[2,2,1,40,640]{4,3,1,0,2:T(8,128)(2,1)S(1)}, bf16[2,2,1,40,640]{4,3,1,0,2:T(8,128)(2,1)S(1)}, u32[]{:S(2)}, u32[]{:S(2)}) collective-permute-start(bf16[2,2,1,40,640]{4,3,1,0,2:T(8,128)(2,1)S(1)} %dynamic-slice_bitcast_fusion.13), channel_id=1, source_target_pairs={{0,1},{1,0},{2,3},{3,2},{4,5},{5,4},{6,7},{7,6},{8,9},{9,8},{10,11... | collective-permute-start | bytes 614408 | tf_op jit(solution)/shard_map/ppermute | solution.py:283
  260.7 44.8 %collective-permute-start.29 = (bf16[2,2,2,2,40,640]{5,4,3,0,1,2:T(8,128)(2,1)S(1)}, bf16[2,2,2,2,40,640]{5,4,3,0,1,2:T(8,128)(2,1)S(1)}, u32[]{:S(2)}, u32[]{:S(2)}) collective-permute-start(bf16[2,2,2,2,40,640]{5,4,3,0,1,2:T(8,128)(2,1)S(1)} %bitcast.321), channel_id=1, source_target_pairs={{0,16},{8,24},{16,0},{24,8},{1,17},{9,25},{17,1},{25,9},{2,18},{10... | collective-permute-start | bytes 2457608 | tf_op jit(solution)/shard_map/ppermute | solution.py:283
  270.1 4.7 %collective-permute-start.11 = (bf16[2,1,40,640]{3,2,0,1:T(8,128)(2,1)S(1)}, bf16[2,1,40,640]{3,2,0,1:T(8,128)(2,1)S(1)}, u32[]{:S(2)}, u32[]{:S(2)}) collective-permute-start(bf16[2,1,40,640]{3,2,0,1:T(8,128)(2,1)S(1)} %dynamic-slice_bitcast_fusion.17), channel_id=1, source_target_pairs={{0,2},{1,3},{2,0},{3,1},{4,6},{5,7},{6,4},{7,5},{8,10},{9,11},{10,... | collective-permute-start | bytes 307208 | tf_op jit(solution)/shard_map/ppermute | solution.py:283
  274.9 5.4 %collective-permute-start.12 = (bf16[1,40,640]{2,1,0:T(8,128)(2,1)S(1)}, bf16[1,40,640]{2,1,0:T(8,128)(2,1)S(1)}, u32[]{:S(2)}, u32[]{:S(2)}) collective-permute-start(bf16[1,40,640]{2,1,0:T(8,128)(2,1)S(1)} %dynamic-slice_bitcast_fusion.18), channel_id=1, source_target_pairs={{0,4},{1,5},{2,6},{3,7},{4,0},{5,1},{6,2},{7,3},{8,12},{9,13},{10,... | collective-permute-start | bytes 153608 | tf_op jit(solution)/shard_map/ppermute | solution.py:283
  277.2 8.2 %collective-permute-start.37 = (bf16[2,3,40,640]{3,2,1,0:T(8,128)(2,1)S(1)}, bf16[2,3,40,640]{3,2,1,0:T(8,128)(2,1)S(1)}, u32[]{:S(2)}, u32[]{:S(2)}) collective-permute-start(bf16[2,3,40,640]{3,2,1,0:T(8,128)(2,1)S(1)} %dynamic-slice_bitcast_fusion.9), channel_id=1, source_target_pairs={{0,2},{1,3},{2,0},{3,1},{4,6},{5,7},{6,4},{7,5},{8,10},{9,11},{10,... | collective-permute-start | bytes 921608 | tf_op jit(solution)/shard_map/ppermute | solution.py:283
  280.3 6.9 %collective-permute-start.13 = (bf16[1,40,640]{2,1,0:T(8,128)(2,1)S(1)}, bf16[1,40,640]{2,1,0:T(8,128)(2,1)S(1)}, u32[]{:S(2)}, u32[]{:S(2)}) collective-permute-start(bf16[1,40,640]{2,1,0:T(8,128)(2,1)S(1)} %fusion.25), channel_id=1, source_target_pairs={{0,16},{8,24},{16,0},{24,8},{1,17},{9,25},{17,1},{25,9},{2,18},{10... | collective-permute-start | bytes 153608 | tf_op jit(solution)/shard_map/ppermute | solution.py:283
  284.1 34.3 %collective-permute-start.22 = (bf16[2,2,2,2,40,640]{5,4,3,0,1,2:T(8,128)(2,1)S(1)}, bf16[2,2,2,2,40,640]{5,4,3,0,1,2:T(8,128)(2,1)S(1)}, u32[]{:S(2)}, u32[]{:S(2)}) collective-permute-start(bf16[2,2,2,2,40,640]{5,4,3,0,1,2:T(8,128)(2,1)S(1)} %bitcast.322), channel_id=1, source_target_pairs={{0,16},{8,24},{16,0},{24,8},{1,17},{9,25},{17,1},{25,9},{2,18},{10... | collective-permute-start | bytes 2457608 | tf_op jit(solution)/shard_map/ppermute | solution.py:283
  285.5 8.1 %collective-permute-start.38 = (bf16[3,40,640]{2,1,0:T(8,128)(2,1)S(1)}, bf16[3,40,640]{2,1,0:T(8,128)(2,1)S(1)}, u32[]{:S(2)}, u32[]{:S(2)}) collective-permute-start(bf16[3,40,640]{2,1,0:T(8,128)(2,1)S(1)} %dynamic-slice_bitcast_fusion.14), channel_id=1, source_target_pairs={{0,4},{1,5},{2,6},{3,7},{4,0},{5,1},{6,2},{7,3},{8,12},{9,13},{10,... | collective-permute-start | bytes 460808 | tf_op jit(solution)/shard_map/ppermute | solution.py:283
  287.3 8.3 %collective-permute-start.14 = (bf16[2,40,640]{2,1,0:T(8,128)(2,1)S(1)}, bf16[2,40,640]{2,1,0:T(8,128)(2,1)S(1)}, u32[]{:S(2)}, u32[]{:S(2)}) collective-permute-start(bf16[2,40,640]{2,1,0:T(8,128)(2,1)S(1)} %maximum_bitcast_fusion.4), channel_id=1, source_target_pairs={{0,8},{8,0},{16,24},{24,16},{1,9},{9,1},{17,25},{25,17},{2,10},{10... | collective-permute-start | bytes 307208 | tf_op jit(solution)/shard_map/ppermute | solution.py:283
  293.6 11.7 %collective-permute-start.39 = (bf16[3,40,640]{2,1,0:T(8,128)(2,1)S(1)}, bf16[3,40,640]{2,1,0:T(8,128)(2,1)S(1)}, u32[]{:S(2)}, u32[]{:S(2)}) collective-permute-start(bf16[3,40,640]{2,1,0:T(8,128)(2,1)S(1)} %fusion.21), channel_id=1, source_target_pairs={{0,16},{8,24},{16,0},{24,8},{1,17},{9,25},{17,1},{25,9},{2,18},{10... | collective-permute-start | bytes 460808 | tf_op jit(solution)/shard_map/ppermute | solution.py:283
  305.4 4.7 %collective-permute-start.40 = (bf16[3,40,640]{2,1,0:T(8,128)(2,1)S(1)}, bf16[3,40,640]{2,1,0:T(8,128)(2,1)S(1)}, u32[]{:S(2)}, u32[]{:S(2)}) collective-permute-start(bf16[3,40,640]{2,1,0:T(8,128)(2,1)S(1)} %add_convert_fusion.2), channel_id=1, source_target_pairs={{0,8},{8,0},{16,24},{24,16},{1,9},{9,1},{17,25},{25,17},{2,10},{10... | collective-permute-start | bytes 460808 | tf_op jit(solution)/shard_map/ppermute | solution.py:283
  305.8 12.3 %collective-permute-start.30 = (bf16[2,2,2,40,640]{4,3,2,0,1:T(8,128)(2,1)S(1)}, bf16[2,2,2,40,640]{4,3,2,0,1:T(8,128)(2,1)S(1)}, u32[]{:S(2)}, u32[]{:S(2)}) collective-permute-start(bf16[2,2,2,40,640]{4,3,2,0,1:T(8,128)(2,1)S(1)} %dynamic-slice_bitcast_fusion.7), channel_id=1, source_target_pairs={{0,1},{1,0},{2,3},{3,2},{4,5},{5,4},{6,7},{7,6},{8,9},{9,8},{10,11... | collective-permute-start | bytes 1228808 | tf_op jit(solution)/shard_map/ppermute | solution.py:283
  308.3 40.6 %collective-permute-start.16 = (bf16[2,2,5,40,640]{4,3,2,1,0:T(8,128)(2,1)S(1)}, bf16[2,2,5,40,640]{4,3,2,1,0:T(8,128)(2,1)S(1)}, u32[]{:S(2)}, u32[]{:S(2)}) collective-permute-start(bf16[2,2,5,40,640]{4,3,2,1,0:T(8,128)(2,1)S(1)} %dynamic-slice_bitcast_fusion.3), channel_id=1, source_target_pairs={{0,1},{1,0},{2,3},{3,2},{4,5},{5,4},{6,7},{7,6},{8,9},{9,8},{10,11... | collective-permute-start | bytes 3072008 | tf_op jit(solution)/shard_map/ppermute | solution.py:283
  318.2 6.4 %collective-permute-start.31 = (bf16[2,2,40,640]{3,2,1,0:T(8,128)(2,1)S(1)}, bf16[2,2,40,640]{3,2,1,0:T(8,128)(2,1)S(1)}, u32[]{:S(2)}, u32[]{:S(2)}) collective-permute-start(bf16[2,2,40,640]{3,2,1,0:T(8,128)(2,1)S(1)} %dynamic-slice_bitcast_fusion.11), channel_id=1, source_target_pairs={{0,2},{1,3},{2,0},{3,1},{4,6},{5,7},{6,4},{7,5},{8,10},{9,11},{10,... | collective-permute-start | bytes 614408 | tf_op jit(solution)/shard_map/ppermute | solution.py:283
  318.7 29.7 %collective-permute-start.23 = (bf16[2,2,2,40,640]{4,3,2,0,1:T(8,128)(2,1)S(1)}, bf16[2,2,2,40,640]{4,3,2,0,1:T(8,128)(2,1)S(1)}, u32[]{:S(2)}, u32[]{:S(2)}) collective-permute-start(bf16[2,2,2,40,640]{4,3,2,0,1:T(8,128)(2,1)S(1)} %dynamic-slice_bitcast_fusion.8), channel_id=1, source_target_pairs={{0,1},{1,0},{2,3},{3,2},{4,5},{5,4},{6,7},{7,6},{8,9},{9,8},{10,11... | collective-permute-start | bytes 1228808 | tf_op jit(solution)/shard_map/ppermute | solution.py:283
  324.7 6.4 %collective-permute-start.32 = (bf16[2,40,640]{2,1,0:T(8,128)(2,1)S(1)}, bf16[2,40,640]{2,1,0:T(8,128)(2,1)S(1)}, u32[]{:S(2)}, u32[]{:S(2)}) collective-permute-start(bf16[2,40,640]{2,1,0:T(8,128)(2,1)S(1)} %dynamic-slice_bitcast_fusion.15), channel_id=1, source_target_pairs={{0,4},{1,5},{2,6},{3,7},{4,0},{5,1},{6,2},{7,3},{8,12},{9,13},{10,... | collective-permute-start | bytes 307208 | tf_op jit(solution)/shard_map/ppermute | solution.py:283
  326.8 21.7 %copy-start.10 = (f32[3,2,40,640]{3,2,0,1:T(8,128)}, f32[3,2,40,640]{3,2,0,1:T(8,128)S(1)}, u32[]{:S(2)}) copy-start(f32[3,2,40,640]{3,2,0,1:T(8,128)S(1)} %convert_bitcast_fusion.2) | copy-start | bytes 1843204
  331.2 17.6 %collective-permute-start.33 = (bf16[2,40,640]{2,1,0:T(8,128)(2,1)S(1)}, bf16[2,40,640]{2,1,0:T(8,128)(2,1)S(1)}, u32[]{:S(2)}, u32[]{:S(2)}) collective-permute-start(bf16[2,40,640]{2,1,0:T(8,128)(2,1)S(1)} %fusion.22), channel_id=1, source_target_pairs={{0,16},{8,24},{16,0},{24,8},{1,17},{9,25},{17,1},{25,9},{2,18},{10... | collective-permute-start | bytes 307208 | tf_op jit(solution)/shard_map/ppermute | solution.py:283
  348.6 8.0 %collective-permute-start.24 = (bf16[2,2,40,640]{3,2,1,0:T(8,128)(2,1)S(1)}, bf16[2,2,40,640]{3,2,1,0:T(8,128)(2,1)S(1)}, u32[]{:S(2)}, u32[]{:S(2)}) collective-permute-start(bf16[2,2,40,640]{3,2,1,0:T(8,128)(2,1)S(1)} %dynamic-slice_bitcast_fusion.12), channel_id=1, source_target_pairs={{0,2},{1,3},{2,0},{3,1},{4,6},{5,7},{6,4},{7,5},{8,10},{9,11},{10,... | collective-permute-start | bytes 614408 | tf_op jit(solution)/shard_map/ppermute | solution.py:283
  348.8 9.9 %collective-permute-start.34 = (bf16[4,40,640]{2,1,0:T(8,128)(2,1)S(1)}, bf16[4,40,640]{2,1,0:T(8,128)(2,1)S(1)}, u32[]{:S(2)}, u32[]{:S(2)}) collective-permute-start(bf16[4,40,640]{2,1,0:T(8,128)(2,1)S(1)} %bitcast.323), channel_id=1, source_target_pairs={{0,8},{8,0},{16,24},{24,16},{1,9},{9,1},{17,25},{25,17},{2,10},{10... | collective-permute-start | bytes 614408 | tf_op jit(solution)/shard_map/ppermute | solution.py:283
  349.3 19.2 %collective-permute-start.17 = (bf16[2,5,40,640]{3,2,1,0:T(8,128)(2,1)S(1)}, bf16[2,5,40,640]{3,2,1,0:T(8,128)(2,1)S(1)}, u32[]{:S(2)}, u32[]{:S(2)}) collective-permute-start(bf16[2,5,40,640]{3,2,1,0:T(8,128)(2,1)S(1)} %dynamic-slice_bitcast_fusion.6), channel_id=1, source_target_pairs={{0,2},{1,3},{2,0},{3,1},{4,6},{5,7},{6,4},{7,5},{8,10},{9,11},{10,... | collective-permute-start | bytes 1536008 | tf_op jit(solution)/shard_map/ppermute | solution.py:283
  356.7 13.0 %collective-permute-start.25 = (bf16[2,40,640]{2,1,0:T(8,128)(2,1)S(1)}, bf16[2,40,640]{2,1,0:T(8,128)(2,1)S(1)}, u32[]{:S(2)}, u32[]{:S(2)}) collective-permute-start(bf16[2,40,640]{2,1,0:T(8,128)(2,1)S(1)} %dynamic-slice_bitcast_fusion.16), channel_id=1, source_target_pairs={{0,4},{1,5},{2,6},{3,7},{4,0},{5,1},{6,2},{7,3},{8,12},{9,13},{10,... | collective-permute-start | bytes 307208 | tf_op jit(solution)/shard_map/ppermute | solution.py:283
  368.7 12.5 %collective-permute-start.18 = (bf16[5,40,640]{2,1,0:T(8,128)(2,1)S(1)}, bf16[5,40,640]{2,1,0:T(8,128)(2,1)S(1)}, u32[]{:S(2)}, u32[]{:S(2)}) collective-permute-start(bf16[5,40,640]{2,1,0:T(8,128)(2,1)S(1)} %dynamic-slice_bitcast_fusion.10), channel_id=1, source_target_pairs={{0,4},{1,5},{2,6},{3,7},{4,0},{5,1},{6,2},{7,3},{8,12},{9,13},{10,... | collective-permute-start | bytes 768008 | tf_op jit(solution)/shard_map/ppermute | solution.py:283
  369.8 12.1 %collective-permute-start.26 = (bf16[2,40,640]{2,1,0:T(8,128)(2,1)S(1)}, bf16[2,40,640]{2,1,0:T(8,128)(2,1)S(1)}, u32[]{:S(2)}, u32[]{:S(2)}) collective-permute-start(bf16[2,40,640]{2,1,0:T(8,128)(2,1)S(1)} %fusion.23), channel_id=1, source_target_pairs={{0,16},{8,24},{16,0},{24,8},{1,17},{9,25},{17,1},{25,9},{2,18},{10... | collective-permute-start | bytes 307208 | tf_op jit(solution)/shard_map/ppermute | solution.py:283
  381.3 8.2 %collective-permute-start.19 = (bf16[5,40,640]{2,1,0:T(8,128)(2,1)S(1)}, bf16[5,40,640]{2,1,0:T(8,128)(2,1)S(1)}, u32[]{:S(2)}, u32[]{:S(2)}) collective-permute-start(bf16[5,40,640]{2,1,0:T(8,128)(2,1)S(1)} %fusion.17), channel_id=1, source_target_pairs={{0,16},{8,24},{16,0},{24,8},{1,17},{9,25},{17,1},{25,9},{2,18},{10... | collective-permute-start | bytes 768008 | tf_op jit(solution)/shard_map/ppermute | solution.py:283
  381.9 7.7 %collective-permute-start.27 = (bf16[4,40,640]{2,1,0:T(8,128)(2,1)S(1)}, bf16[4,40,640]{2,1,0:T(8,128)(2,1)S(1)}, u32[]{:S(2)}, u32[]{:S(2)}) collective-permute-start(bf16[4,40,640]{2,1,0:T(8,128)(2,1)S(1)} %bitcast.324), channel_id=1, source_target_pairs={{0,8},{8,0},{16,24},{24,16},{1,9},{9,1},{17,25},{25,17},{2,10},{10... | collective-permute-start | bytes 614408 | tf_op jit(solution)/shard_map/ppermute | solution.py:283
  389.5 1.6 collective-permute-start.20
  (28 other events, 173.8 us)
